TPU v7x, 128 devices: a whole 4x4x4 slice. The times are simulated.
128 devices in a mesh: wave: 32 (over x, y, core), lev: 4 (over z).
Axes of the slice: x: 4, y: 4, z: 4, core: 2. Of those that a mesh axis runs over, the one named last changes fastest.
Arguments:
- spec_in: bfloat16 [320, 2, 4, 128, 1281], P('wave', None, None, 'lev'), may hold values from -6 to 6
- legendre: bfloat16 [320, 1281, 256], P('wave'), may hold values from -0.15625 to 0.15625
- lat_weight: float32 [256], replicated, may hold values from 0.5 to 2
- vertical_matrix: bfloat16 [128, 128], replicated, may hold values from -0.5 to 0.5
- pair_table: int32 [320], replicated, may hold values from 0 to 639, as said below
Outputs:
- spec_out: bfloat16 [320, 2, 4, 128, 1281], P('wave', None, None, 'lev')
Inputs may be any that keep to these rules, and one draw needn't show every extreme that they name: Slot s holds the wavenumbers pair_table[s] and 1279 - pair_table[s]; the values are distinct.
All inputs are finite; a program needn't handle non-finite values.
Results may differ from a plain program's by a relative error of at most 0.0075.
Values may be sent and summed in bfloat16 or wider, within the bound.
No kernel may reach another device: no remote copies, remote signals or barrier semaphores. Data moves between devices by JAX's collectives and lax.ppermute only.
A program may use at most 128 MiB of HBM per device.

v0:
```python
import math

import jax
import jax.numpy as jnp
from jax import lax
from jax.experimental import pallas as pl
from jax.experimental.pallas import tpu as pltpu
from jax.sharding import PartitionSpec as P

MW = 1280
NLON = 2688
FLD = 4
PLEN = 1281
NLAT = 256
SLOTS = 10
LV = 32
SRC = 32
KA = 704
KB = 768
KLAST = 672
F32 = jnp.float32
BF16 = jnp.bfloat16
VMEM_LIMIT = 56 * 1024 * 1024


def dot(a, b):
    return lax.dot_general(a, b, (((1,), (0,)), ((), ())), preferred_element_type=F32)


def dot_t(a, b):
    return lax.dot_general(a, b, (((1,), (1,)), ((), ())), preferred_element_type=F32)


def swap_matrix(outer, inner):
    n = outer * inner
    row = lax.broadcasted_iota(jnp.int32, (n, n), 0)
    col = lax.broadcasted_iota(jnp.int32, (n, n), 1)
    source = (row % outer) * inner + row // outer
    return jnp.where(col == source, 1.0, 0.0).astype(F32).astype(BF16)


def inverse_kernel(pairs, spec, leg, out, store):
    s = pl.program_id(0)
    p = pairs[s]
    edge = MW - p
    parity = p & 1
    coeff = spec[0].reshape(2 * FLD * LV, PLEN)
    rows = lax.broadcasted_iota(jnp.int32, (768, 1), 0) + 512
    first = rows < edge
    middle = leg[0, 512:1280, :]
    zero = jnp.zeros((), BF16)
    f0 = dot(coeff[:, 0:512], leg[0, 0:512, :]) + dot(
        coeff[:, 512:1280], jnp.where(first, middle, zero)
    )
    f1 = dot(coeff[:, 512:1280], jnp.where(first, zero, middle)) + coeff[:, 1280:1281].astype(
        F32
    ) * leg[0, 1280:1281, :].astype(F32)
    for h, f in enumerate((f0, f1)):
        e = jnp.bitwise_xor(parity, h)
        half = f.astype(BF16)
        for c in range(2):
            store[2 * e + c, s] = half[c * 128 : (c + 1) * 128].reshape(FLD, LV, NLAT)

    def swapped(tile, blocks):
        perm = swap_matrix(8, LV)
        for f in range(FLD):
            rows8 = blocks(f)
            moved = dot(perm, rows8).reshape(LV, 8, NLAT).astype(BF16)
            out[:, tile, :, f * NLAT : (f + 1) * NLAT] = moved

    @pl.when(s == 7)
    def _():
        for q in range(4):
            swapped(q, lambda f: store[q, 0:8, f].reshape(8 * LV, NLAT))

    @pl.when(s == 9)
    def _():
        swapped(
            4,
            lambda f: jnp.concatenate([store[q, 8 + i, f] for i in range(2) for q in range(4)], 0),
        )


def inverse_legendre(pairs, spec_in, legendre):
    return pl.pallas_call(
        inverse_kernel,
        grid=(SLOTS,),
        in_specs=[
            pl.BlockSpec(memory_space=pltpu.SMEM),
            pl.BlockSpec((1, 2, FLD, LV, PLEN), lambda s: (s, 0, 0, 0, 0)),
            pl.BlockSpec((1, PLEN, NLAT), lambda s: (s, 0, 0)),
        ],
        out_specs=pl.BlockSpec((SRC, 5, 8, FLD * NLAT), lambda s: (0, 0, 0, 0)),
        out_shape=jax.ShapeDtypeStruct((SRC, 5, 8, FLD * NLAT), BF16),
        scratch_shapes=[pltpu.VMEM((4, SLOTS, FLD, LV, NLAT), BF16)],
        compiler_params=pltpu.CompilerParams(vmem_limit_bytes=VMEM_LIMIT),
        cost_estimate=pl.CostEstimate(
            flops=6_000_000_000, bytes_accessed=17_000_000, transcendentals=0
        ),
    )(pairs, spec_in, legendre)


def small_tables(pair_table):
    pairs = pair_table.reshape(SRC, SLOTS)
    pure = pairs[:, :8].reshape(1, 256)
    mixed = jnp.repeat(pairs[:, 8:10], 4, axis=1).reshape(1, 256)
    both = jnp.broadcast_to(jnp.concatenate([pure, mixed], 1), (4, 512))
    q = jnp.arange(4, dtype=jnp.int32)[:, None]
    even_odd, part = q // 2, q % 2
    column = jnp.arange(512, dtype=jnp.int32)[None, :]
    own = (column < 256) | (column % 4 == q)
    wave = jnp.where(both % 2 == even_odd, both, MW - 1 - both)
    wave = wave.reshape(2048)
    shift = jnp.broadcast_to(part * (NLON // 4), (4, 512)).reshape(2048)
    amp = jnp.where(own, F32(1.0 / math.sqrt(MW)), F32(0.0)).reshape(2048)

    def angles(index):
        return (index % NLON).astype(F32) * F32(2.0 * math.pi / NLON)

    coarse = jnp.arange(KA // 64, dtype=jnp.int32)[:, None] * 64
    fine = jnp.arange(64, dtype=jnp.int32)[:, None]
    a1 = angles(coarse * wave[None, :])
    a2 = angles(fine * wave[None, :] + shift[None, :])
    rows = (jnp.cos(a1), jnp.sin(a1), jnp.cos(a2) * amp[None, :], jnp.sin(a2) * amp[None, :])
    coarse = jnp.arange(KB // 128, dtype=jnp.int32)[None, :] * 128
    fine = jnp.arange(128, dtype=jnp.int32)[None, :]
    b1 = angles(coarse * wave[:, None])
    b2 = angles(fine * wave[:, None] + shift[:, None])
    columns = (jnp.cos(b1), jnp.sin(b1), jnp.cos(b2) * amp[:, None], jnp.sin(b2) * amp[:, None])
    return rows, columns


def table_kernel(ca, sa, cb, sb, da, ea, db, eb, inv, direct):
    for a in range(KA // 64):
        value = ca[a : a + 1, :] * cb[...] - sa[a : a + 1, :] * sb[...]
        if a == KA // 64 - 1:
            k = lax.broadcasted_iota(jnp.int32, (64, 1), 0) + a * 64
            value = jnp.where(k <= KLAST, value, 0.0)
        inv[0, a * 64 : (a + 1) * 64, :] = value.astype(BF16)
    for a in range(KB // 128):
        value = da[:, a : a + 1] * db[...] - ea[:, a : a + 1] * eb[...]
        if a == 0 or (a + 1) * 128 > KLAST:
            k = lax.broadcasted_iota(jnp.int32, (1, 128), 1) + a * 128
            ends = (k == 0) | (k == KLAST)
            value = value * jnp.where(ends, 0.5, jnp.where(k <= KLAST, 1.0, 0.0))
        direct[0, :, a * 128 : (a + 1) * 128] = value.astype(BF16)


def wave_tables(pair_table):
    rows, columns = small_tables(pair_table)
    row_specs = [
        pl.BlockSpec((r.shape[0], 512), lambda q: (0, q)) for r in rows
    ]
    col_specs = [pl.BlockSpec((512, c.shape[1]), lambda q: (q, 0)) for c in columns]
    return pl.pallas_call(
        table_kernel,
        grid=(4,),
        in_specs=row_specs + col_specs,
        out_specs=[
            pl.BlockSpec((1, KA, 512), lambda q: (q, 0, 0)),
            pl.BlockSpec((1, 512, KB), lambda q: (q, 0, 0)),
        ],
        out_shape=[
            jax.ShapeDtypeStruct((4, KA, 512), BF16),
            jax.ShapeDtypeStruct((4, 512, KB), BF16),
        ],
        compiler_params=pltpu.CompilerParams(vmem_limit_bytes=32 * 1024 * 1024),
        cost_estimate=pl.CostEstimate(
            flops=12_000_000, bytes_accessed=9_000_000, transcendentals=0
        ),
    )(*rows, *columns)


def grid_kernel(recv, inv, direct, out2, outr, x, v):
    for t in range(5):
        tile = recv[:, t].astype(F32).reshape(256, FLD * NLAT).astype(BF16)
        if t < 4:
            x[t, 0:256, :] = tile
        else:
            for q in range(4):
                x[q, 256:512, :] = tile
    for q in range(4):
        v[q, KA:KB, :] = jnp.zeros((KB - KA, FLD * NLAT), BF16)
    step = KA // 4

    def body(i, carry):
        k = pl.ds(pl.multiple_of(i * step, 16), step)
        grids = []
        for f in range(FLD):
            lanes = slice(f * NLAT, (f + 1) * NLAT)
            ec, es, oc, os_ = [dot(inv[q, k, :], x[q, :, lanes]) for q in range(4)]
            e_plus, e_minus, o_plus, o_minus = ec + es, ec - es, oc + os_, oc - os_
            grids.append((e_plus + o_plus, e_minus + o_minus, e_plus - o_plus, e_minus - o_minus))
        for f in range(FLD):
            lanes = slice(f * NLAT, (f + 1) * NLAT)
            t0, t1, t2, t3 = [
                g + 0.5 * g * n for g, n in zip(grids[f], grids[(f + 1) % FLD])
            ]
            e_plus, o_plus, e_minus, o_minus = t0 + t2, t0 - t2, t1 + t3, t1 - t3
            v[0, k, lanes] = (e_plus + e_minus).astype(BF16)
            v[1, k, lanes] = (e_plus - e_minus).astype(BF16)
            v[2, k, lanes] = (o_plus + o_minus).astype(BF16)
            v[3, k, lanes] = (o_plus - o_minus).astype(BF16)
        return carry

    lax.fori_loop(0, 4, body, 0)
    scale = MW / NLON

    def put(f, tile, value):
        value = (value * scale).reshape(SRC, 8, NLAT).astype(BF16)
        if f == 2:
            out2[:, tile] = value
        else:
            place = {0: 0, 1: 1, 3: 2}[f]
            outr[:, tile, :, place * NLAT : (place + 1) * NLAT] = value

    for f in range(FLD):
        lanes = slice(f * NLAT, (f + 1) * NLAT)
        mixed = None
        for q in range(4):
            put(f, q, dot(direct[q, 0:256, :], v[q, :, lanes]))
            term = dot(direct[q, 256:512, :], v[q, :, lanes])
            mixed = term if mixed is None else mixed + term
        put(f, 4, mixed)


def grid_step(received, inv, direct):
    return pl.pallas_call(
        grid_kernel,
        out_shape=[
            jax.ShapeDtypeStruct((SRC, 5, 8, NLAT), BF16),
            jax.ShapeDtypeStruct((SRC, 5, 8, 3 * NLAT), BF16),
        ],
        scratch_shapes=[
            pltpu.VMEM((4, 512, FLD * NLAT), BF16),
            pltpu.VMEM((4, KB, FLD * NLAT), BF16),
        ],
        compiler_params=pltpu.CompilerParams(vmem_limit_bytes=VMEM_LIMIT),
        cost_estimate=pl.CostEstimate(
            flops=7_000_000_000, bytes_accessed=12_000_000, transcendentals=0
        ),
    )(received, inv, direct)


def unswap(recv, lanes, write):
    perm = swap_matrix(LV, 8)
    for t in range(5):
        tile = recv[:, t, :, lanes].astype(F32).reshape(8 * LV, NLAT).astype(BF16)
        moved = dot(perm, tile).astype(BF16).reshape(8, LV, NLAT)
        for r in range(8):
            if t < 4:
                write(t, r, moved[r])
            else:
                write(r % 4, 8 + r // 4, moved[r])


def thermal_kernel(recv, out):
    def write(q, s, value):
        out[q, s] = value

    unswap(recv, slice(0, NLAT), write)


def thermal_rows(received):
    return pl.pallas_call(
        thermal_kernel,
        out_shape=jax.ShapeDtypeStruct((4, SLOTS, LV, NLAT), BF16),
        compiler_params=pltpu.CompilerParams(vmem_limit_bytes=16 * 1024 * 1024),
        cost_estimate=pl.CostEstimate(
            flops=170_000_000, bytes_accessed=1_400_000, transcendentals=0
        ),
    )(received)


def link_kernel(matrix, r0, r1, r2, r3, o0, o1, o2, o3):
    for s in range(SLOTS):
        column = jnp.concatenate([r[s] for r in (r0, r1, r2, r3)], 0)
        result = dot(matrix[...], column).astype(BF16)
        for i, o in enumerate((o0, o1, o2, o3)):
            o[s] = result[i * LV : (i + 1) * LV]


def vertical_link(rows, vertical_matrix):
    me = lax.axis_index("lev")
    double = jnp.concatenate([vertical_matrix, vertical_matrix], 0)
    rolled = lax.dynamic_slice_in_dim(double, me * LV, 4 * LV, 0)
    double = jnp.concatenate([rolled, rolled], 1)
    rolled = lax.dynamic_slice_in_dim(double, me * LV, 4 * LV, 1)

    def moved(value, shift):
        if shift == 0:
            return value
        return lax.ppermute(value, "lev", [(i, (i + shift) % 4) for i in range(4)])

    def chunk(shift):
        return lax.dynamic_index_in_dim(rows, (me + shift) % 4, 0, keepdims=False)

    order = (1, 3, 2, 0)
    got = {shift: moved(chunk(shift), shift) for shift in order}
    relative = [got[(-i) % 4] for i in range(4)]
    shape = jax.ShapeDtypeStruct((SLOTS, LV, NLAT), BF16)
    linked = pl.pallas_call(
        link_kernel,
        out_shape=[shape] * 4,
        compiler_params=pltpu.CompilerParams(vmem_limit_bytes=16 * 1024 * 1024),
        cost_estimate=pl.CostEstimate(
            flops=90_000_000, bytes_accessed=1_400_000, transcendentals=0
        ),
    )(rolled, *relative)
    back = {shift: moved(linked[shift], shift) for shift in order}
    return [back[shift] for shift in range(4)]


def direct_kernel(scalars, recv, rows2, c0, c1, c2, c3, leg, weight, out, store, coupled):
    s = pl.program_id(0)

    @pl.when(s == 0)
    def _():
        me = scalars[SLOTS]
        for shift, c in enumerate((c0, c1, c2, c3)):
            coupled[lax.rem(me - shift + 4, 4)] = c[...]
        for place in range(3):
            def write(q, slot, value):
                store[place, q, slot] = value

            unswap(recv, slice(place * NLAT, (place + 1) * NLAT), write)

    p = scalars[s]
    edge = MW - p
    parity = p & 1
    weighted = (leg[0].astype(F32) * weight[...] * math.sqrt(PLEN / NLAT)).astype(BF16)

    def left(h):
        e = jnp.bitwise_xor(parity, h)
        blocks = []
        for c in range(2):
            q = 2 * e + c
            blocks += [
                store[0, q, s], store[1, q, s], rows2[q, s], store[2, q, s], coupled[q, s]
            ]
        return jnp.concatenate(blocks, 0)

    l0, l1 = left(0), left(1)

    def finish(value, r0, width):
        r = lax.broadcasted_iota(jnp.int32, (1, width), 1) + r0
        degree = jnp.where(r < edge, p + r, r - 1).astype(F32)
        implicit = degree * (degree + 1.0) / float(MW * (MW - 1))
        value = value.reshape(2, FLD + 1, LV, width)
        for c in range(2):
            out[0, c, 0, :, r0 : r0 + width] = (
                value[c, 0] - implicit * value[c, 4]
            ).astype(BF16)
            for f in range(1, FLD):
                out[0, c, f, :, r0 : r0 + width] = value[c, f].astype(BF16)

    for r0 in range(0, 1280, 256):
        w = weighted[r0 : r0 + 256]
        value = dot_t(l0, w)
        if r0 >= 512:
            r = lax.broadcasted_iota(jnp.int32, (1, 256), 1) + r0
            value = jnp.where(r < edge, value, dot_t(l1, w))
        finish(value, r0, 256)
    last = jnp.sum(
        l1.astype(F32) * weighted[1280:1281].astype(F32), axis=1, keepdims=True
    )
    finish(last, 1280, 1)


def direct_legendre(scalars, received, rows2, coupled, legendre, lat_weight):
    whole = lambda a: pl.BlockSpec(a.shape, lambda s: (0,) * a.ndim)
    return pl.pallas_call(
        direct_kernel,
        grid=(SLOTS,),
        in_specs=[pl.BlockSpec(memory_space=pltpu.SMEM), whole(received), whole(rows2)]
        + [whole(c) for c in coupled]
        + [pl.BlockSpec((1, PLEN, NLAT), lambda s: (s, 0, 0)), whole(lat_weight)],
        out_specs=pl.BlockSpec((1, 2, FLD, LV, PLEN), lambda s: (s, 0, 0, 0, 0)),
        out_shape=jax.ShapeDtypeStruct((SLOTS, 2, FLD, LV, PLEN), BF16),
        scratch_shapes=[
            pltpu.VMEM((3, 4, SLOTS, LV, NLAT), BF16),
            pltpu.VMEM((4, SLOTS, LV, NLAT), BF16),
        ],
        compiler_params=pltpu.CompilerParams(vmem_limit_bytes=VMEM_LIMIT),
        cost_estimate=pl.CostEstimate(
            flops=7_000_000_000, bytes_accessed=17_000_000, transcendentals=0
        ),
    )(scalars, received, rows2, *coupled, legendre, lat_weight)


def exchange(value):
    return lax.all_to_all(value, "wave", split_axis=0, concat_axis=0, tiled=True)


def local(spec_in, legendre, lat_weight, vertical_matrix, pair_table):
    pairs = lax.dynamic_slice_in_dim(pair_table, lax.axis_index("wave") * SLOTS, SLOTS)
    sent = inverse_legendre(pairs, spec_in, legendre)
    received = exchange(sent)
    inv, direct = wave_tables(pair_table)
    back2, back_rest = grid_step(received, inv, direct)
    arrived2 = exchange(back2)
    arrived_rest = exchange(back_rest)
    rows2 = thermal_rows(arrived2)
    coupled = vertical_link(rows2, vertical_matrix)
    scalars = jnp.concatenate([pairs, lax.axis_index("lev").reshape(1)]).astype(jnp.int32)
    return direct_legendre(
        scalars, arrived_rest, rows2, coupled, legendre, lat_weight.reshape(1, NLAT)
    )


def solution(mesh):
    return jax.shard_map(
        local,
        mesh=mesh,
        in_specs=(P("wave", None, None, "lev", None), P("wave", None, None), P(), P(), P()),
        out_specs=P("wave", None, None, "lev", None),
        check_vma=False,
    )
```

profile of v0, /device:TPU:1, one launch (start us, length us, event | category | flops | bytes accessed | tf_op | source)
XLA Modules:
  0.0 133.6 jit_solution(14324564976239379664)
XLA Ops:
  0.0 1.3 dynamic_slice.22.pairs
  1.3 12.4 %shard_map.55 = bf16[32,5,8,1024]{3,2,1,0:T(8,128)(2,1)} custom-call(s32[10]{0:T(128)} %dynamic_slice.22.pairs, bf16[10,2,4,32,1281]{4,3,2,1,0:T(8,128)(2,1)} %spec.1, bf16[10,1281,256]{2,1,0:T(8,128)(2,1)} %leg.3), custom_call_target="tpu_custom_call" | custom-call | flops 6000000000 | bytes 17000000 | tf_op jit(solution)/shard_map/pallas_call | solution.py:85
  13.7 8.8 %all-to-all-start = ((bf16[32,5,8,1024]{3,2,1,0:T(8,128)(2,1)}), bf16[32,5,8,1024]{3,2,1,0:T(8,128)(2,1)}, u32[]{:S(2)}, u32[]{:S(2)}) async-start(bf16[32,5,8,1024]{3,2,1,0:T(8,128)(2,1)} %shard_map.55), calls=%async_computation | async-start | bytes 5242880 | tf_op jit(solution)/shard_map/all_to_all | solution.py:392
  22.8 0.1 reshape_reshape.3
  23.2 0.1 fusion.17
  23.3 0.4 copy.6
  23.7 0.6 fusion.14
  24.3 2.2 %sine_multiply_fusion.1 = (f32[64,2048]{1,0:T(8,128)S(1)}, f32[64,2048]{1,0:T(8,128)S(1)}) fusion(f32[2048]{0:T(1024)S(1)} %bitcast.28, s32[2048]{0:T(1024)S(1)} %bitcast.26, s32[2048]{0:T(1024)S(1)} %bitcast.23), kind=kLoop, calls=%fused_computation.14 | loop fusion | flops 1572864 | bytes 1073152 | tf_op jit(solution)/shard_map/mul | solution.py:124
  26.6 4.5 %sine_multiply_fusion = (f32[2048,128]{1,0:T(8,128)S(1)}, f32[2048,128]{1,0:T(8,128)S(1)}) fusion(f32[2048]{0:T(1024)S(1)} %bitcast.29, s32[2048]{0:T(1024)S(1)} %bitcast.27, s32[2048]{0:T(1024)S(1)} %bitcast.24), kind=kLoop, calls=%fused_computation.3 | loop fusion | flops 3145728 | bytes 2121728 | tf_op jit(solution)/shard_map/mul | solution.py:129
  31.0 3.7 %multiply_sine_fusion = (f32[2048,6]{1,0:T(8,128)S(1)}, f32[2048,6]{1,0:T(8,128)S(1)}) fusion(f32[2048,6]{1,0:T(8,128)S(1)} %copy.6), kind=kLoop, calls=%fused_computation.9 | loop fusion | flops 12288 | bytes 147456 | tf_op jit(solution)/shard_map/sin | solution.py:129
  34.8 4.3 %shard_map.56 = (bf16[4,704,512]{2,1,0:T(8,128)(2,1)S(1)}, bf16[4,512,768]{2,1,0:T(8,128)(2,1)S(1)}) custom-call(f32[11,2048]{1,0:T(8,128)S(1)} %get-tuple-element.34.ca, f32[11,2048]{1,0:T(8,128)S(1)} %get-tuple-element.33.sa, f32[64,2048]{1,0:T(8,128)S(1)} %get-tuple-element.32.cb, f32[64,2048]{1,0:T(8,128)S(1)} %get-tuple-element.31.sb, ...), custom_call_target="tpu_custom_call" | custom-call | flops 12000000 | bytes 9000000 | tf_op jit(solution)/shard_map/pallas_call | solution.py:155
  39.1 1.7 %copy-done.1 = bf16[4,512,768]{2,1,0:T(8,128)(2,1)} copy-done((bf16[4,512,768]{2,1,0:T(8,128)(2,1)}, bf16[4,512,768]{2,1,0:T(8,128)(2,1)S(1)}, u32[]{:S(2)}) %copy-start.1) | copy-done | bytes 3145752
  40.8 1.6 %copy-done.2 = bf16[4,704,512]{2,1,0:T(8,128)(2,1)} copy-done((bf16[4,704,512]{2,1,0:T(8,128)(2,1)}, bf16[4,704,512]{2,1,0:T(8,128)(2,1)S(1)}, u32[]{:S(2)}) %copy-start.2) | copy-done | bytes 2883608
  42.3 14.1 %all-to-all-done.recv = bf16[32,5,8,1024]{3,2,1,0:T(8,128)(2,1)} async-done(((bf16[32,5,8,1024]{3,2,1,0:T(8,128)(2,1)}), bf16[32,5,8,1024]{3,2,1,0:T(8,128)(2,1)}, u32[]{:S(2)}, u32[]{:S(2)}) %all-to-all-start) | async-done | bytes 2621472 | tf_op jit(solution)/shard_map/all_to_all | solution.py:392
  56.4 14.9 %shard_map.57 = (bf16[32,5,8,256]{3,2,1,0:T(8,128)(2,1)}, bf16[32,5,8,768]{3,2,1,0:T(8,128)(2,1)}) custom-call(bf16[32,5,8,1024]{3,2,1,0:T(8,128)(2,1)} %all-to-all-done.recv, bf16[4,704,512]{2,1,0:T(8,128)(2,1)} %copy-done.2, bf16[4,512,768]{2,1,0:T(8,128)(2,1)} %copy-done.1), custom_call_target="tpu_custom_call" | custom-call | flops 7000000000 | bytes 12000000 | tf_op jit(solution)/shard_map/pallas_call | solution.py:228
  71.3 17.6 %all_to_all.15.recv = bf16[32,5,8,256]{3,2,1,0:T(8,128)(2,1)S(1)} all-to-all(bf16[32,5,8,256]{3,2,1,0:T(8,128)(2,1)} %get-tuple-element.16), channel_id=1, replica_groups=mesh['wave'=32,'lev'=4] {'wave'}, dimensions={0} | all-to-all | bytes 1310720 | tf_op jit(solution)/shard_map/all_to_all | solution.py:392
  88.9 3.9 %all-to-all-start.1 = ((bf16[32,5,8,768]{3,2,1,0:T(8,128)(2,1)}), bf16[32,5,8,768]{3,2,1,0:T(8,128)(2,1)S(1)}, u32[]{:S(2)}, u32[]{:S(2)}) async-start(bf16[32,5,8,768]{3,2,1,0:T(8,128)(2,1)} %get-tuple-element.15), calls=%async_computation.1 | async-start | bytes 3932160 | tf_op jit(solution)/shard_map/all_to_all | solution.py:392
  92.9 0.3 shard_map.58.rows2
  93.3 3.8 %collective-permute-start = (bf16[10,32,256]{2,1,0:T(8,128)(2,1)S(1)}, bf16[10,32,256]{2,1,0:T(8,128)(2,1)S(1)}, u32[]{:S(2)}, u32[]{:S(2)}) collective-permute-start(bf16[10,32,256]{2,1,0:T(8,128)(2,1)S(1)} %get-tuple-element.27), channel_id=1, source_target_pairs={{0,3},{1,0},{2,1},{3,2},{4,7},{5,4},{6,5},{7,6},{8,11},{9,8},{10,9... | collective-permute-start | bytes 491528 | tf_op jit(solution)/shard_map/ppermute | solution.py:293
  97.1 0.7 collective-permute-start.2
  97.8 0.1 fusion.22
  98.1 6.0 %collective-permute-done.r1 = bf16[10,32,256]{2,1,0:T(8,128)(2,1)S(1)} collective-permute-done((bf16[10,32,256]{2,1,0:T(8,128)(2,1)S(1)}, bf16[10,32,256]{2,1,0:T(8,128)(2,1)S(1)}, u32[]{:S(2)}, u32[]{:S(2)}) %collective-permute-start) | collective-permute-done | bytes 163872 | tf_op jit(solution)/shard_map/ppermute | solution.py:293
  104.1 3.6 %collective-permute-done.2.r3 = bf16[10,32,256]{2,1,0:T(8,128)(2,1)S(1)} collective-permute-done((bf16[10,32,256]{2,1,0:T(8,128)(2,1)S(1)}, bf16[10,32,256]{2,1,0:T(8,128)(2,1)S(1)}, u32[]{:S(2)}, u32[]{:S(2)}) %collective-permute-start.2) | collective-permute-done | bytes 163872 | tf_op jit(solution)/shard_map/ppermute | solution.py:293
  107.7 0.3 shard_map.59
  108.0 0.7 copy-done.3
  108.7 1.3 collective-permute-start.4
  110.0 1.4 %collective-permute-start.5 = (bf16[10,32,256]{2,1,0:T(8,128)(2,1)S(1)}, bf16[10,32,256]{2,1,0:T(8,128)(2,1)S(1)}, u32[]{:S(2)}, u32[]{:S(2)}) collective-permute-start(bf16[10,32,256]{2,1,0:T(8,128)(2,1)S(1)} %get-tuple-element.20), channel_id=1, source_target_pairs={{0,3},{1,0},{2,1},{3,2},{4,7},{5,4},{6,5},{7,6},{8,11},{9,8},{10,9... | collective-permute-start | bytes 491528 | tf_op jit(solution)/shard_map/ppermute | solution.py:293
  111.4 0.6 pad_add_fusion.1.scalars
  112.0 6.8 %collective-permute-done.3.c1 = bf16[10,32,256]{2,1,0:T(8,128)(2,1)S(1)} collective-permute-done((bf16[10,32,256]{2,1,0:T(8,128)(2,1)S(1)}, bf16[10,32,256]{2,1,0:T(8,128)(2,1)S(1)}, u32[]{:S(2)}, u32[]{:S(2)}) %collective-permute-start.3) | collective-permute-done | bytes 163872 | tf_op jit(solution)/shard_map/ppermute | solution.py:293
  118.8 0.8 all-to-all-done.1.recv
  119.6 1.3 copy-done.4
  120.9 12.7 %shard_map.60 = bf16[10,2,4,32,1281]{4,3,2,1,0:T(8,128)(2,1)} custom-call(s32[11]{0:T(128)} %pad_add_fusion.1.scalars, bf16[32,5,8,768]{3,2,1,0:T(8,128)(2,1)} %copy-done.4, bf16[4,10,32,256]{3,2,1,0:T(8,128)(2,1)} %copy-done, bf16[10,32,256]{2,1,0:T(8,128)(2,1)} %copy-done.3, bf16[10,32,256]{2,1,0:T(8,128)(2,1)} %copy-done.7, ...), custom_call_target="tpu_custom_call" | custom-call | flops 7000000000 | bytes 17000000 | tf_op jit(solution)/shard_map/pallas_call | solution.py:372
  (43 shorter events, 0.8 us)
Async XLA Ops:
  13.7 8.8 %copy-start.6 = (s32[320]{0:T(512)S(1)}, s32[320]{0:T(512)}, u32[]{:S(2)}) copy-start(s32[320]{0:T(512)} %param.9) | copy-start | bytes 3844
  13.7 42.7 %all-to-all-start = ((bf16[32,5,8,1024]{3,2,1,0:T(8,128)(2,1)}), bf16[32,5,8,1024]{3,2,1,0:T(8,128)(2,1)}, u32[]{:S(2)}, u32[]{:S(2)}) async-start(bf16[32,5,8,1024]{3,2,1,0:T(8,128)(2,1)} %shard_map.55), calls=%async_computation | async-start | bytes 5242880 | tf_op jit(solution)/shard_map/all_to_all | solution.py:392
  39.1 1.7 %copy-start.1 = (bf16[4,512,768]{2,1,0:T(8,128)(2,1)}, bf16[4,512,768]{2,1,0:T(8,128)(2,1)S(1)}, u32[]{:S(2)}) copy-start(bf16[4,512,768]{2,1,0:T(8,128)(2,1)S(1)} %get-tuple-element.14.direct) | copy-start | bytes 9437188
  40.8 1.6 %copy-start.2 = (bf16[4,704,512]{2,1,0:T(8,128)(2,1)}, bf16[4,704,512]{2,1,0:T(8,128)(2,1)S(1)}, u32[]{:S(2)}) copy-start(bf16[4,704,512]{2,1,0:T(8,128)(2,1)S(1)} %get-tuple-element.13.inv) | copy-start | bytes 8650756
  88.9 8.9 %copy-start.5 = (bf16[128,128]{1,0:T(8,128)(2,1)S(1)}, bf16[128,128]{1,0:T(8,128)(2,1)}, u32[]{:S(2)}) copy-start(bf16[128,128]{1,0:T(8,128)(2,1)} %param.8) | copy-start | bytes 98308
  88.9 22.5 %copy-start.10 = (s32[10]{0:T(128)S(1)}, s32[10]{0:T(128)}, u32[]{:S(2)}) copy-start(s32[10]{0:T(128)} %dynamic_slice.22.pairs) | copy-start | bytes 124
  88.9 30.7 %all-to-all-start.1 = ((bf16[32,5,8,768]{3,2,1,0:T(8,128)(2,1)}), bf16[32,5,8,768]{3,2,1,0:T(8,128)(2,1)S(1)}, u32[]{:S(2)}, u32[]{:S(2)}) async-start(bf16[32,5,8,768]{3,2,1,0:T(8,128)(2,1)} %get-tuple-element.15), calls=%async_computation.1 | async-start | bytes 3932160 | tf_op jit(solution)/shard_map/all_to_all | solution.py:392
  93.2 26.4 %copy-start = (bf16[4,10,32,256]{3,2,1,0:T(8,128)(2,1)}, bf16[4,10,32,256]{3,2,1,0:T(8,128)(2,1)S(1)}, u32[]{:S(2)}) copy-start(bf16[4,10,32,256]{3,2,1,0:T(8,128)(2,1)S(1)} %shard_map.58.rows2) | copy-start | bytes 1966084
  93.3 10.8 %collective-permute-start = (bf16[10,32,256]{2,1,0:T(8,128)(2,1)S(1)}, bf16[10,32,256]{2,1,0:T(8,128)(2,1)S(1)}, u32[]{:S(2)}, u32[]{:S(2)}) collective-permute-start(bf16[10,32,256]{2,1,0:T(8,128)(2,1)S(1)} %get-tuple-element.27), channel_id=1, source_target_pairs={{0,3},{1,0},{2,1},{3,2},{4,7},{5,4},{6,5},{7,6},{8,11},{9,8},{10,9... | collective-permute-start | bytes 491528 | tf_op jit(solution)/shard_map/ppermute | solution.py:293
  97.1 7.0 %collective-permute-start.1 = (bf16[10,32,256]{2,1,0:T(8,128)(2,1)S(1)}, bf16[10,32,256]{2,1,0:T(8,128)(2,1)S(1)}, u32[]{:S(2)}, u32[]{:S(2)}) collective-permute-start(bf16[10,32,256]{2,1,0:T(8,128)(2,1)S(1)} %get-tuple-element.26), channel_id=1, source_target_pairs={{0,2},{1,3},{2,0},{3,1},{4,6},{5,7},{6,4},{7,5},{8,10},{9,11},{10,... | collective-permute-start | bytes 491528 | tf_op jit(solution)/shard_map/ppermute | solution.py:293
  97.1 10.6 %collective-permute-start.2 = (bf16[10,32,256]{2,1,0:T(8,128)(2,1)S(1)}, bf16[10,32,256]{2,1,0:T(8,128)(2,1)S(1)}, u32[]{:S(2)}, u32[]{:S(2)}) collective-permute-start(bf16[10,32,256]{2,1,0:T(8,128)(2,1)S(1)} %get-tuple-element.25), channel_id=1, source_target_pairs={{0,1},{1,2},{2,3},{3,0},{4,5},{5,6},{6,7},{7,4},{8,9},{9,10},{10,1... | collective-permute-start | bytes 491528 | tf_op jit(solution)/shard_map/ppermute | solution.py:293
  108.0 0.7 copy-start.3
  108.7 10.1 %collective-permute-start.3 = (bf16[10,32,256]{2,1,0:T(8,128)(2,1)S(1)}, bf16[10,32,256]{2,1,0:T(8,128)(2,1)S(1)}, u32[]{:S(2)}, u32[]{:S(2)}) collective-permute-start(bf16[10,32,256]{2,1,0:T(8,128)(2,1)S(1)} %get-tuple-element.18), channel_id=1, source_target_pairs={{0,1},{1,2},{2,3},{3,0},{4,5},{5,6},{6,7},{7,4},{8,9},{9,10},{10,1... | collective-permute-start | bytes 491528 | tf_op jit(solution)/shard_map/ppermute | solution.py:293
  108.7 10.1 %collective-permute-start.4 = (bf16[10,32,256]{2,1,0:T(8,128)(2,1)S(1)}, bf16[10,32,256]{2,1,0:T(8,128)(2,1)S(1)}, u32[]{:S(2)}, u32[]{:S(2)}) collective-permute-start(bf16[10,32,256]{2,1,0:T(8,128)(2,1)S(1)} %get-tuple-element.19), channel_id=1, source_target_pairs={{0,2},{1,3},{2,0},{3,1},{4,6},{5,7},{6,4},{7,5},{8,10},{9,11},{10,... | collective-permute-start | bytes 491528 | tf_op jit(solution)/shard_map/ppermute | solution.py:293
  110.0 8.8 %collective-permute-start.5 = (bf16[10,32,256]{2,1,0:T(8,128)(2,1)S(1)}, bf16[10,32,256]{2,1,0:T(8,128)(2,1)S(1)}, u32[]{:S(2)}, u32[]{:S(2)}) collective-permute-start(bf16[10,32,256]{2,1,0:T(8,128)(2,1)S(1)} %get-tuple-element.20), channel_id=1, source_target_pairs={{0,3},{1,0},{2,1},{3,2},{4,7},{5,4},{6,5},{7,6},{8,11},{9,8},{10,9... | collective-permute-start | bytes 491528 | tf_op jit(solution)/shard_map/ppermute | solution.py:293
  118.8 0.8 copy-start.7
  118.8 0.8 copy-start.8
  118.8 0.8 copy-start.9
  119.6 1.3 copy-start.4
where the time goes:
time: 134 us
  Pallas kernels  45 us (34%)
  waiting for transfers between devices  31.3 us (23%)
  starting transfers between devices  19.9 us (15%)
  blocking collectives  17.6 us (13%)
  other arithmetic  12.1 us (9%)
  local copies, waits for them, and re-layouts  7.41 us (6%)
    all_to_all x1, blocking collectives, exchange(): lax.all_to_all(value, 'wave', split_axis=0, concat_axis=0, tiled=True)  17.6 us
    ppermute x6, waiting for transfers between devices, moved(): return lax.ppermute(value, 'lev', [(i, (i + shift) % 4) for i in range(4)])  16.4 us
    pallas_call x1, Pallas kernels, grid_step(): pl.pallas_call(grid_kernel, out_shape=[jax.ShapeDtypeStruct((SRC, 5, 8, N...  14.9 us
    all_to_all x2, waiting for transfers between devices, exchange(): lax.all_to_all(value, 'wave', split_axis=0, concat_axis=0, tiled=True)  14.8 us
    pallas_call x1, Pallas kernels, direct_legendre(): pl.pallas_call(direct_kernel, grid=(SLOTS,), in_specs=[pl.BlockSpec(memor...  12.7 us
    all_to_all x2, starting transfers between devices, exchange(): lax.all_to_all(value, 'wave', split_axis=0, concat_axis=0, tiled=True)  12.7 us
    pallas_call x1, Pallas kernels, inverse_legendre(): pl.pallas_call(inverse_kernel, grid=(SLOTS,), in_specs=[pl.BlockSpec(memo...  12.4 us
    ppermute x6, starting transfers between devices, moved(): return lax.ppermute(value, 'lev', [(i, (i + shift) % 4) for i in range(4)])  7.21 us
  transfers between devices with their start and end apart: 8, of which 5 were waited for; matrix products, arithmetic and copies ran while one was open for 10% of the time, Pallas kernels for 4%

commit v1 on v0

v1 whole, which is shorter than its diff:
```python
import functools
import math

import jax
import jax.numpy as jnp
from jax import lax
from jax.experimental import pallas as pl
from jax.experimental.pallas import tpu as pltpu
from jax.sharding import PartitionSpec as P

MW = 1280
NLON = 2688
FLD = 4
PLEN = 1281
NLAT = 256
SLOTS = 10
LV = 32
SRC = 32
KA = 704
KB = 768
KLAST = 672
F32 = jnp.float32
BF16 = jnp.bfloat16
MIB = 1024 * 1024
VM = pl.BlockSpec(memory_space=pltpu.VMEM)


def in_hbm(a):
    return pltpu.with_memory_space_constraint(a, pltpu.HBM)


def dot(a, b):
    return lax.dot_general(a, b, (((1,), (0,)), ((), ())), preferred_element_type=F32)


def dot_t(a, b):
    return lax.dot_general(a, b, (((1,), (1,)), ((), ())), preferred_element_type=F32)


def swap_matrix(outer, inner):
    n = outer * inner
    row = lax.broadcasted_iota(jnp.int32, (n, n), 0)
    col = lax.broadcasted_iota(jnp.int32, (n, n), 1)
    source = (row % outer) * inner + row // outer
    return jnp.where(col == source, 1.0, 0.0).astype(F32).astype(BF16)


def inverse_kernel(pairs, spec, leg, out, coeffs, legs, store, moved, sem, out_sem):
    base = lax.axis_index("wave") * SLOTS
    window = 5

    def copies(s):
        return (
            pltpu.make_async_copy(spec.at[s], coeffs.at[s], sem.at[0, s]),
            pltpu.make_async_copy(leg.at[s], legs.at[s], sem.at[1, s]),
        )

    def start(s):
        for copy in copies(s):
            copy.start()

    for s in range(window):
        start(s)

    def step(s, carry):
        @pl.when(s + window < SLOTS)
        def _():
            start(s + window)

        for copy in copies(s):
            copy.wait()
        p = pairs[base + s]
        edge = MW - p
        parity = p & 1
        coeff = coeffs[s].reshape(2 * FLD * LV, PLEN)
        column = lax.broadcasted_iota(jnp.int32, (1, 768), 1) + 512
        first = jnp.where(column < edge, 1.0, 0.0).astype(BF16)
        second = jnp.where(column < edge, 0.0, 1.0).astype(BF16)
        middle = coeff[:, 512:1280]
        both = dot(
            jnp.concatenate([middle * first, middle * second], 0), legs[s, 512:1280, :]
        )
        last = coeff[:, 1280:1281].astype(F32) * legs[s, 1280:1281, :].astype(F32)
        halves = (both[:256] + dot(coeff[:, 0:512], legs[s, 0:512, :]), both[256:] + last)
        for h in range(2):
            e = jnp.bitwise_xor(parity, h)
            half = halves[h].astype(BF16)
            for c in range(2):
                store[2 * e + c, s] = half[c * 128 : (c + 1) * 128].reshape(FLD, LV, NLAT)
        return carry

    perm = swap_matrix(8, LV)
    leave = [
        pltpu.make_async_copy(moved.at[t], out.at[:, t], out_sem.at[t]) for t in range(5)
    ]

    def swapped(tile, blocks):
        for f in range(FLD):
            value = dot(perm, blocks(f)).reshape(LV, 8, NLAT).astype(BF16)
            moved[tile, :, :, f * NLAT : (f + 1) * NLAT] = value
        leave[tile].start()

    lax.fori_loop(0, 8, step, 0)
    for q in range(4):
        swapped(q, lambda f: store[q, 0:8, f].reshape(8 * LV, NLAT))
    lax.fori_loop(8, SLOTS, step, 0)
    swapped(
        4, lambda f: jnp.concatenate([store[q, 8 + i, f] for i in range(2) for q in range(4)], 0)
    )
    for t in range(5):
        leave[t].wait()


def inverse_legendre(pair_table, spec_in, legendre):
    return pl.pallas_call(
        inverse_kernel,
        in_specs=[pl.BlockSpec(memory_space=pltpu.SMEM)]
        + [pl.BlockSpec(memory_space=pl.ANY)] * 2,
        out_specs=pl.BlockSpec(memory_space=pl.ANY),
        out_shape=pltpu.HBM((SRC, 5, 8, FLD * NLAT), BF16),
        scratch_shapes=[
            pltpu.VMEM((SLOTS, 2, FLD, LV, PLEN), BF16),
            pltpu.VMEM((SLOTS, PLEN, NLAT), BF16),
            pltpu.VMEM((4, SLOTS, FLD, LV, NLAT), BF16),
            pltpu.VMEM((5, SRC, 8, FLD * NLAT), BF16),
            pltpu.SemaphoreType.DMA((2, SLOTS)),
            pltpu.SemaphoreType.DMA((5,)),
        ],
        compiler_params=pltpu.CompilerParams(vmem_limit_bytes=32 * MIB),
        cost_estimate=pl.CostEstimate(
            flops=6_000_000_000, bytes_accessed=17_000_000, transcendentals=0
        ),
    )(in_hbm(pair_table), in_hbm(spec_in), in_hbm(legendre))


def small_tables(pair_table):
    pairs = pair_table.reshape(SRC, SLOTS)
    pure = pairs[:, :8].reshape(1, 256)
    mixed = jnp.repeat(pairs[:, 8:10], 4, axis=1).reshape(1, 256)
    both = jnp.broadcast_to(jnp.concatenate([pure, mixed], 1), (4, 512))
    q = jnp.arange(4, dtype=jnp.int32)[:, None]
    even_odd, part = q // 2, q % 2
    column = jnp.arange(512, dtype=jnp.int32)[None, :]
    own = (column < 256) | (column % 4 == q)
    wave = jnp.where(both % 2 == even_odd, both, MW - 1 - both)
    wave = wave.reshape(2048)
    shift = jnp.broadcast_to(part * (NLON // 4), (4, 512)).reshape(2048)
    amp = jnp.where(own, F32(1.0 / math.sqrt(MW)), F32(0.0)).reshape(2048)

    def angles(index):
        return (index % NLON).astype(F32) * F32(2.0 * math.pi / NLON)

    coarse = jnp.arange(KA // 64, dtype=jnp.int32)[:, None] * 64
    fine = jnp.arange(64, dtype=jnp.int32)[:, None]
    a1 = angles(coarse * wave[None, :])
    a2 = angles(fine * wave[None, :] + shift[None, :])
    rows = (jnp.cos(a1), jnp.sin(a1), jnp.cos(a2) * amp[None, :], jnp.sin(a2) * amp[None, :])
    coarse = jnp.arange(KB // 128, dtype=jnp.int32)[None, :] * 128
    fine = jnp.arange(128, dtype=jnp.int32)[None, :]
    b1 = angles(coarse * wave[:, None])
    b2 = angles(fine * wave[:, None] + shift[:, None])
    columns = (jnp.cos(b1), jnp.sin(b1), jnp.cos(b2) * amp[:, None], jnp.sin(b2) * amp[:, None])
    return rows, columns


def table_kernel(ca, sa, cb, sb, da, ea, db, eb, leg, weight, inv, direct, weighted):
    weighted[0] = (leg[0].astype(F32) * weight[...] * math.sqrt(PLEN / NLAT)).astype(BF16)

    @pl.when(pl.program_id(0) < 4)
    def _():
        for a in range(KA // 64):
            value = ca[a : a + 1, :] * cb[...] - sa[a : a + 1, :] * sb[...]
            if a == KA // 64 - 1:
                k = lax.broadcasted_iota(jnp.int32, (64, 1), 0) + a * 64
                value = jnp.where(k <= KLAST, value, 0.0)
            inv[0, a * 64 : (a + 1) * 64, :] = value.astype(BF16)
        for a in range(KB // 128):
            value = da[:, a : a + 1] * db[...] - ea[:, a : a + 1] * eb[...]
            if a == 0 or (a + 1) * 128 > KLAST:
                k = lax.broadcasted_iota(jnp.int32, (1, 128), 1) + a * 128
                ends = (k == 0) | (k == KLAST)
                value = value * jnp.where(ends, 0.5, jnp.where(k <= KLAST, 1.0, 0.0))
            direct[0, :, a * 128 : (a + 1) * 128] = value.astype(BF16)


def all_tables(pair_table, legendre, lat_weight):
    rows, columns = small_tables(pair_table)
    group = lambda s: jnp.minimum(s, 3)
    row_specs = [pl.BlockSpec((r.shape[0], 512), lambda s: (0, group(s))) for r in rows]
    col_specs = [pl.BlockSpec((512, c.shape[1]), lambda s: (group(s), 0)) for c in columns]
    slot_spec = pl.BlockSpec((1, PLEN, NLAT), lambda s: (s, 0, 0))
    return pl.pallas_call(
        table_kernel,
        grid=(SLOTS,),
        in_specs=row_specs
        + col_specs
        + [slot_spec, pl.BlockSpec((1, NLAT), lambda s: (0, 0))],
        out_specs=[
            pl.BlockSpec((1, KA, 512), lambda s: (group(s), 0, 0)),
            pl.BlockSpec((1, 512, KB), lambda s: (group(s), 0, 0)),
            slot_spec,
        ],
        out_shape=[
            pltpu.HBM((4, KA, 512), BF16),
            pltpu.HBM((4, 512, KB), BF16),
            pltpu.HBM((SLOTS, PLEN, NLAT), BF16),
        ],
        compiler_params=pltpu.CompilerParams(vmem_limit_bytes=24 * MIB),
        cost_estimate=pl.CostEstimate(
            flops=20_000_000, bytes_accessed=26_000_000, transcendentals=0
        ),
    )(*rows, *columns, in_hbm(legendre), lat_weight.reshape(1, NLAT))


def grid_kernel(needed, wanted, recv, inv_any, direct_any, out, inv, direct, x, v, sem):
    get_inv = [
        pltpu.make_async_copy(inv_any.at[q], inv.at[q], sem.at[0, q]) for q in range(4)
    ]
    get_direct = [
        pltpu.make_async_copy(direct_any.at[q], direct.at[q], sem.at[1, q]) for q in range(4)
    ]
    for copy in get_inv + get_direct:
        copy.start()
    for t in range(5):
        for i in range(len(needed)):
            lanes = slice(i * NLAT, (i + 1) * NLAT)
            f = needed[i]
            tile = recv[:, t, :, f * NLAT : (f + 1) * NLAT].astype(F32)
            tile = tile.reshape(256, NLAT).astype(BF16)
            for q in range(4) if t == 4 else (t,):
                row = 256 if t == 4 else 0
                x[q, row : row + 256, lanes] = tile
    sums = {}
    for q in range(4):
        get_inv[q].wait()
        for i, f in enumerate(needed):
            sums[f, q] = dot(inv[q], x[q, :, i * NLAT : (i + 1) * NLAT])
    grids = {}
    for f in needed:
        ec, es, oc, os_ = [sums[f, q] for q in range(4)]
        e_plus, e_minus, o_plus, o_minus = ec + es, ec - es, oc + os_, oc - os_
        grids[f] = (e_plus + o_plus, e_minus + o_minus, e_plus - o_plus, e_minus - o_minus)
    for q in range(4):
        get_direct[q].wait()
    scale = MW / NLON
    for i, f in enumerate(wanted):
        lanes = slice(i * NLAT, (i + 1) * NLAT)
        t0, t1, t2, t3 = [g + 0.5 * g * n for g, n in zip(grids[f], grids[(f + 1) % FLD])]
        e_plus, o_plus, e_minus, o_minus = t0 + t2, t0 - t2, t1 + t3, t1 - t3
        v[0, 0:KA, lanes] = (e_plus + e_minus).astype(BF16)
        v[1, 0:KA, lanes] = (e_plus - e_minus).astype(BF16)
        v[2, 0:KA, lanes] = (o_plus + o_minus).astype(BF16)
        v[3, 0:KA, lanes] = (o_plus - o_minus).astype(BF16)
        mixed = None
        for q in range(4):
            v[q, KA:KB, lanes] = jnp.zeros((KB - KA, NLAT), BF16)
            pure = dot(direct[q, 0:256, :], v[q, :, lanes]) * scale
            out[:, q, :, lanes] = pure.reshape(SRC, 8, NLAT).astype(BF16)
            term = dot(direct[q, 256:512, :], v[q, :, lanes])
            mixed = term if mixed is None else mixed + term
        out[:, 4, :, lanes] = (mixed * scale).reshape(SRC, 8, NLAT).astype(BF16)


def grid_step(needed, wanted, received, inv, direct):
    return pl.pallas_call(
        functools.partial(grid_kernel, needed, wanted),
        in_specs=[VM] + [pl.BlockSpec(memory_space=pl.ANY)] * 2,
        out_specs=VM,
        out_shape=pltpu.HBM((SRC, 5, 8, len(wanted) * NLAT), BF16),
        scratch_shapes=[
            pltpu.VMEM((4, KA, 512), BF16),
            pltpu.VMEM((4, 512, KB), BF16),
            pltpu.VMEM((4, 512, len(needed) * NLAT), BF16),
            pltpu.VMEM((4, KB, len(wanted) * NLAT), BF16),
            pltpu.SemaphoreType.DMA((2, 4)),
        ],
        compiler_params=pltpu.CompilerParams(vmem_limit_bytes=(12 + 8 * len(wanted)) * MIB),
        cost_estimate=pl.CostEstimate(
            flops=2_000_000_000 * len(wanted), bytes_accessed=9_000_000, transcendentals=0
        ),
    )(received, in_hbm(inv), in_hbm(direct))


def unswap(recv, lanes, write):
    perm = swap_matrix(LV, 8)
    for t in range(5):
        tile = recv[:, t, :, lanes].astype(F32).reshape(8 * LV, NLAT).astype(BF16)
        moved = dot(perm, tile).astype(BF16).reshape(8, LV, NLAT)
        for r in range(8):
            if t < 4:
                write(t, r, moved[r])
            else:
                write(r % 4, 8 + r // 4, moved[r])


def thermal_kernel(recv, out):
    def write(q, s, value):
        out[q, s] = value

    unswap(recv, slice(0, NLAT), write)


def thermal_rows(received):
    return pl.pallas_call(
        thermal_kernel,
        out_shape=jax.ShapeDtypeStruct((4, SLOTS, LV, NLAT), BF16),
        compiler_params=pltpu.CompilerParams(vmem_limit_bytes=16 * MIB),
        cost_estimate=pl.CostEstimate(
            flops=170_000_000, bytes_accessed=1_400_000, transcendentals=0
        ),
    )(received)


def link_kernel(matrix, r0, r1, r2, r3, o0, o1, o2, o3):
    for s in range(SLOTS):
        column = jnp.concatenate([r[s] for r in (r0, r1, r2, r3)], 0)
        result = dot(matrix[...], column).astype(BF16)
        for i, o in enumerate((o0, o1, o2, o3)):
            o[s] = result[i * LV : (i + 1) * LV]


def vertical_link(rows, vertical_matrix):
    me = lax.axis_index("lev")
    double = jnp.concatenate([vertical_matrix, vertical_matrix], 0)
    rolled = lax.dynamic_slice_in_dim(double, me * LV, 4 * LV, 0)
    double = jnp.concatenate([rolled, rolled], 1)
    rolled = lax.dynamic_slice_in_dim(double, me * LV, 4 * LV, 1)

    def moved(value, shift):
        if shift == 0:
            return value
        return lax.ppermute(value, "lev", [(i, (i + shift) % 4) for i in range(4)])

    def chunk(shift):
        return lax.dynamic_index_in_dim(rows, (me + shift) % 4, 0, keepdims=False)

    order = (1, 3, 2, 0)
    got = {shift: moved(chunk(shift), shift) for shift in order}
    relative = [got[(-i) % 4] for i in range(4)]
    shape = jax.ShapeDtypeStruct((SLOTS, LV, NLAT), BF16)
    linked = pl.pallas_call(
        link_kernel,
        out_shape=[shape] * 4,
        compiler_params=pltpu.CompilerParams(vmem_limit_bytes=16 * MIB),
        cost_estimate=pl.CostEstimate(
            flops=90_000_000, bytes_accessed=1_400_000, transcendentals=0
        ),
    )(rolled, *relative)
    back = {shift: moved(linked[shift], shift) for shift in order}
    return [back[shift] for shift in range(4)]


def edge_of(pairs, s):
    p = pairs[lax.axis_index("wave") * SLOTS + s]
    return p, MW - p, p & 1


def legendre_rows(edge, left, weighted, give, mend):
    for r0 in range(0, 1280, 256):
        half = 0 if r0 < 512 else (r0 >= edge).astype(jnp.int32)
        give(r0, 256, dot_t(left(half), weighted(r0, 256)))
    left1 = left(1)
    row = weighted(1280, 1).astype(F32)
    give(1280, 1, jnp.sum(left1.astype(F32) * row, axis=1, keepdims=True))
    r0 = pl.multiple_of(jnp.minimum(edge // 256, 4) * 256, 256)
    r = lax.broadcasted_iota(jnp.int32, (1, 256), 1) + r0
    mend(r0, r < edge, dot_t(left1, weighted(r0, 256)))


def over_slots(weight, table, sem, before, slot, leave):
    window = 4

    def arrive(s):
        return pltpu.make_async_copy(weight.at[s], table.at[s], sem.at[s])

    for s in range(window):
        arrive(s).start()
    before()

    def step(s, carry):
        @pl.when(s + window < SLOTS)
        def _():
            arrive(s + window).start()

        arrive(s).wait()
        slot(s, lambda r0, width: table[s, pl.ds(r0, width), :])
        for copy in leave(s):
            copy.start()
        return carry

    lax.fori_loop(0, SLOTS, step, 0)
    for s in range(SLOTS):
        for copy in leave(s):
            copy.wait()


def thermal_result_kernel(pairs, rows2, weight, out, table, stage, sem, out_sem):
    def leave(s):
        return [
            pltpu.make_async_copy(stage.at[s, c], out.at[s, c, 2], out_sem.at[s, c])
            for c in range(2)
        ]

    def slot(s, weighted):
        p, edge, parity = edge_of(pairs, s)

        def left(h):
            q = 2 * jnp.bitwise_xor(parity, h)
            return jnp.concatenate([rows2[q, s], rows2[q + 1, s]], 0)

        def give(r0, width, value):
            value = value.reshape(2, LV, width).astype(BF16)
            stage[s, :, :, r0 : r0 + width] = value

        def mend(r0, keep, value):
            lanes = pl.ds(r0, 256)
            value = jnp.where(keep, stage[s, :, :, lanes].astype(F32), value.reshape(2, LV, 256))
            stage[s, :, :, lanes] = value.astype(BF16)

        legendre_rows(edge, left, weighted, give, mend)

    over_slots(weight, table, sem, lambda: None, slot, leave)


def thermal_result(pair_table, rows2, weighted):
    return pl.pallas_call(
        thermal_result_kernel,
        in_specs=[
            pl.BlockSpec(memory_space=pltpu.SMEM), VM, pl.BlockSpec(memory_space=pl.ANY)
        ],
        out_specs=pl.BlockSpec(memory_space=pl.ANY),
        out_shape=jax.ShapeDtypeStruct((SLOTS, 2, FLD, LV, PLEN), BF16),
        scratch_shapes=[
            pltpu.VMEM((SLOTS, PLEN, NLAT), BF16),
            pltpu.VMEM((SLOTS, 2, LV, PLEN), BF16),
            pltpu.SemaphoreType.DMA((SLOTS,)),
            pltpu.SemaphoreType.DMA((SLOTS, 2)),
        ],
        compiler_params=pltpu.CompilerParams(vmem_limit_bytes=20 * MIB),
        cost_estimate=pl.CostEstimate(
            flops=2_000_000_000, bytes_accessed=9_000_000, transcendentals=0
        ),
    )(pair_table, rows2, in_hbm(weighted))


def rest_kernel(pairs, recv, c0, c1, c2, c3, weight, begun, out, store, table, stage, sem, out_sem):
    def before():
        me = lax.axis_index("lev")
        for shift, c in enumerate((c0, c1, c2, c3)):
            store[3, lax.rem(me - shift + 4, 4)] = c[...]
        for place in range(3):
            def write(q, slot, value):
                store[place, q, slot] = value

            unswap(recv, slice(place * NLAT, (place + 1) * NLAT), write)

    def leave(s):
        return [
            pltpu.make_async_copy(
                stage.at[s, c, pl.ds(0, 2)], out.at[s, c, pl.ds(0, 2)], out_sem.at[s, c, 0]
            )
            for c in range(2)
        ] + [
            pltpu.make_async_copy(stage.at[s, c, 2], out.at[s, c, 3], out_sem.at[s, c, 1])
            for c in range(2)
        ]

    def slot(s, weighted):
        p, edge, parity = edge_of(pairs, s)

        def left(h):
            q = 2 * jnp.bitwise_xor(parity, h)
            return jnp.concatenate([store[f, q + c, s] for c in range(2) for f in range(4)], 0)

        def corrected(r0, width, value):
            r = lax.broadcasted_iota(jnp.int32, (1, width), 1) + r0
            degree = jnp.where(r < edge, p + r, r - 1).astype(F32)
            implicit = degree * (degree + 1.0) / float(MW * (MW - 1))
            value = value.reshape(2, 4, LV, width)
            return [
                [value[c, 0] - implicit * value[c, 3], value[c, 1], value[c, 2]] for c in range(2)
            ]

        def give(r0, width, value):
            for c, fields in enumerate(corrected(r0, width, value)):
                for f in range(3):
                    stage[s, c, f, :, r0 : r0 + width] = fields[f].astype(BF16)

        def mend(r0, keep, value):
            lanes = pl.ds(r0, 256)
            for c, fields in enumerate(corrected(r0, 256, value)):
                for f in range(3):
                    kept = stage[s, c, f, :, lanes].astype(F32)
                    stage[s, c, f, :, lanes] = jnp.where(keep, kept, fields[f]).astype(BF16)

        legendre_rows(edge, left, weighted, give, mend)

    over_slots(weight, table, sem, before, slot, leave)


def rest_result(pair_table, received, coupled, weighted, begun):
    return pl.pallas_call(
        rest_kernel,
        in_specs=[pl.BlockSpec(memory_space=pltpu.SMEM)]
        + [VM] * 5
        + [pl.BlockSpec(memory_space=pl.ANY)] * 2,
        out_specs=pl.BlockSpec(memory_space=pl.ANY),
        out_shape=jax.ShapeDtypeStruct((SLOTS, 2, FLD, LV, PLEN), BF16),
        input_output_aliases={7: 0},
        scratch_shapes=[
            pltpu.VMEM((4, 4, SLOTS, LV, NLAT), BF16),
            pltpu.VMEM((SLOTS, PLEN, NLAT), BF16),
            pltpu.VMEM((SLOTS, 2, 3, LV, PLEN), BF16),
            pltpu.SemaphoreType.DMA((SLOTS,)),
            pltpu.SemaphoreType.DMA((SLOTS, 2, 2)),
        ],
        compiler_params=pltpu.CompilerParams(vmem_limit_bytes=24 * MIB),
        cost_estimate=pl.CostEstimate(
            flops=5_000_000_000, bytes_accessed=15_000_000, transcendentals=0
        ),
    )(pair_table, received, *coupled, in_hbm(weighted), in_hbm(begun))


def exchange(value):
    return lax.all_to_all(value, "wave", split_axis=0, concat_axis=0, tiled=True)


def local(spec_in, legendre, lat_weight, vertical_matrix, pair_table):
    sent = inverse_legendre(pair_table, spec_in, legendre)
    received = exchange(sent)
    inv, direct, weighted = all_tables(pair_table, legendre, lat_weight)
    arrived2 = exchange(grid_step((2, 3), (2,), received, inv, direct))
    arrived_rest = exchange(grid_step((0, 1, 2, 3), (0, 1, 3), received, inv, direct))
    rows2 = thermal_rows(arrived2)
    coupled = vertical_link(rows2, vertical_matrix)
    begun = thermal_result(pair_table, rows2, weighted)
    return rest_result(pair_table, arrived_rest, coupled, weighted, begun)


def solution(mesh):
    return jax.shard_map(
        local,
        mesh=mesh,
        in_specs=(P("wave", None, None, "lev", None), P("wave", None, None), P(), P(), P()),
        out_specs=P("wave", None, None, "lev", None),
        check_vma=False,
    )
```

time: 134 us -> 115 us (0.86)
  blocking collectives: 17.6 us -> 0 us
  waiting for transfers between devices: 31.3 us -> 20.4 us
  Pallas kernels: 45 us -> 52.8 us
  starting transfers between devices: 19.9 us -> 27.6 us
  local copies, waits for them, and re-layouts: 7.41 us -> 1.97 us
    all_to_all x1 -> x0, blocking collectives: 17.6 us -> none  [exchange(): lax.all_to_all(value, 'wave', split_axis=0, concat_axis=0, tiled=True)]
    ppermute x6, waiting for transfers between devices: 16.4 us -> 7.53 us  [moved(): return lax.ppermute(value, 'lev', [(i, (i + shift) % 4) for i in range(4)])]
    pallas_call x4 -> x6, Pallas kernels: 44.4 us -> 52.1 us  [the longest x2 16.7 us: grid_step(): pl.pallas_call(functools.partial(grid_kernel, needed, wanted), in_specs=[...]
    all_to_all x2 -> x3, starting transfers between devices: 12.7 us -> 18.1 us  [exchange(): lax.all_to_all(value, 'wave', split_axis=0, concat_axis=0, tiled=True)]
    unnamed x26 -> x12, local copies, waits for them, and re-layouts: 5.25 us -> 0.1 us
    ppermute x6, starting transfers between devices: 7.21 us -> 9.51 us  [moved(): return lax.ppermute(value, 'lev', [(i, (i + shift) % 4) for i in range(4)])]
    all_to_all x2 -> x3, waiting for transfers between devices: 14.8 us -> 12.9 us  [exchange(): lax.all_to_all(value, 'wave', split_axis=0, concat_axis=0, tiled=True)]
  transfers between devices with their start and end apart: 8 -> 9, of which waited for: 5 -> 6; matrix products, arithmetic and copies ran while one was open for 10% -> 12% of each run, Pallas kernels for 4% -> 26%
where the time goes in v1:
time: 115 us
  Pallas kernels  52.8 us (46%)
  starting transfers between devices  27.6 us (24%)
  waiting for transfers between devices  20.4 us (18%)
  other arithmetic  11.5 us (10%)
  local copies, waits for them, and re-layouts  1.97 us (2%)
    all_to_all x3, starting transfers between devices, exchange(): lax.all_to_all(value, 'wave', split_axis=0, concat_axis=0, tiled=True)  18.1 us
    pallas_call x2, Pallas kernels, grid_step(): pl.pallas_call(functools.partial(grid_kernel, needed, wanted), in_specs=[...  16.7 us
    all_to_all x3, waiting for transfers between devices, exchange(): lax.all_to_all(value, 'wave', split_axis=0, concat_axis=0, tiled=True)  12.9 us
    pallas_call x1, Pallas kernels, all_tables(): pl.pallas_call(table_kernel, grid=(SLOTS,), in_specs=row_specs + col_spec...  12.7 us
    ppermute x6, starting transfers between devices, moved(): return lax.ppermute(value, 'lev', [(i, (i + shift) % 4) for i in range(4)])  9.51 us
    pallas_call x1, Pallas kernels, inverse_legendre(): pl.pallas_call(inverse_kernel, in_specs=[pl.BlockSpec(memory_space=pltpu....  8.66 us
    pallas_call x1, Pallas kernels, rest_result(): pl.pallas_call(rest_kernel, in_specs=[pl.BlockSpec(memory_space=pltpu.SME...  7.76 us
    ppermute x6, waiting for transfers between devices, moved(): return lax.ppermute(value, 'lev', [(i, (i + shift) % 4) for i in range(4)])  7.53 us
  transfers between devices with their start and end apart: 9, of which 6 were waited for; matrix products, arithmetic and copies ran while one was open for 12% of the time, Pallas kernels for 26%

profile of v1, /device:TPU:1, one launch (start us, length us, event | category | flops | bytes accessed | tf_op | source)
XLA Modules:
  0.0 114.8 jit_solution(17028633766171716222)
XLA Ops:
  0.0 8.7 %shard_map.55 = bf16[32,5,8,1024]{3,2,1,0:T(8,128)(2,1)} custom-call(s32[320]{0:T(512)} %pairs.5, bf16[10,2,4,32,1281]{4,3,2,1,0:T(8,128)(2,1)} %spec.1, bf16[10,1281,256]{2,1,0:T(8,128)(2,1)} %leg.3), custom_call_target="tpu_custom_call" | custom-call | flops 6000000000 | bytes 17000000 | tf_op jit(solution)/shard_map/pallas_call | solution.py:115
  8.7 8.6 %all-to-all-start = ((bf16[32,5,8,1024]{3,2,1,0:T(8,128)(2,1)}), bf16[32,5,8,1024]{3,2,1,0:T(8,128)(2,1)S(1)}, u32[]{:S(2)}, u32[]{:S(2)}) async-start(bf16[32,5,8,1024]{3,2,1,0:T(8,128)(2,1)} %shard_map.55), calls=%async_computation | async-start | bytes 5242880 | tf_op jit(solution)/shard_map/all_to_all | solution.py:525
  17.8 0.1 reshape_reshape.3
  18.1 0.1 fusion.17
  18.2 1.3 %copy.7 = f32[2048,6]{1,0:T(8,128)} copy(f32[2048,6]{0,1:T(8,128)S(1)} %fusion.17) | data formatting | bytes 98304 | tf_op jit(solution)/shard_map/convert_element_type | solution.py:151
  19.5 0.6 fusion.14
  20.2 2.2 %sine_multiply_fusion.1 = (f32[64,2048]{1,0:T(8,128)S(1)}, f32[64,2048]{1,0:T(8,128)S(1)}) fusion(f32[2048]{0:T(1024)S(1)} %bitcast.26, s32[2048]{0:T(1024)S(1)} %bitcast.28, s32[2048]{0:T(1024)S(1)} %bitcast.23), kind=kLoop, calls=%fused_computation.14 | loop fusion | flops 1572864 | bytes 1073152 | tf_op jit(solution)/shard_map/mul | solution.py:157
  22.4 4.5 %sine_multiply_fusion = (f32[2048,128]{1,0:T(8,128)S(1)}, f32[2048,128]{1,0:T(8,128)S(1)}) fusion(f32[2048]{0:T(1024)S(1)} %bitcast.27, s32[2048]{0:T(1024)S(1)} %bitcast.29, s32[2048]{0:T(1024)S(1)} %bitcast.24), kind=kLoop, calls=%fused_computation.3 | loop fusion | flops 3145728 | bytes 2121728 | tf_op jit(solution)/shard_map/mul | solution.py:162
  26.9 3.7 %multiply_sine_fusion = (f32[2048,6]{1,0:T(8,128)S(1)}, f32[2048,6]{1,0:T(8,128)S(1)}) fusion(f32[2048,6]{1,0:T(8,128)S(1)} %copy-done.2), kind=kLoop, calls=%fused_computation.9 | loop fusion | flops 12288 | bytes 147456 | tf_op jit(solution)/shard_map/sin | solution.py:162
  30.6 12.7 %shard_map.56 = (bf16[4,704,512]{2,1,0:T(8,128)(2,1)}, bf16[4,512,768]{2,1,0:T(8,128)(2,1)}, bf16[10,1281,256]{2,1,0:T(8,128)(2,1)}) custom-call(f32[11,2048]{1,0:T(8,128)S(1)} %get-tuple-element.32.ca, f32[11,2048]{1,0:T(8,128)S(1)} %get-tuple-element.31.sa, f32[64,2048]{1,0:T(8,128)S(1)} %get-tuple-element.30.cb, f32[64,2048]{1,0:T(8,128)S(1)} %get-tuple-element.29.sb, ...), custom_call_target="tpu_custom_call" | custom-call | flops 20000000 | bytes 26000000 | tf_op jit(solution)/shard_map/pallas_call | solution.py:192
  43.3 7.9 %all-to-all-done.recv = bf16[32,5,8,1024]{3,2,1,0:T(8,128)(2,1)S(1)} async-done(((bf16[32,5,8,1024]{3,2,1,0:T(8,128)(2,1)}), bf16[32,5,8,1024]{3,2,1,0:T(8,128)(2,1)S(1)}, u32[]{:S(2)}, u32[]{:S(2)}) %all-to-all-start) | async-done | bytes 2621472 | tf_op jit(solution)/shard_map/all_to_all | solution.py:525
  51.2 6.2 %shard_map.58 = bf16[32,5,8,256]{3,2,1,0:T(8,128)(2,1)} custom-call(bf16[32,5,8,1024]{3,2,1,0:T(8,128)(2,1)S(1)} %all-to-all-done.recv, bf16[4,704,512]{2,1,0:T(8,128)(2,1)} %get-tuple-element.12.inv_any, bf16[4,512,768]{2,1,0:T(8,128)(2,1)} %get-tuple-element.13.direct_any), custom_call_target="tpu_custom_call" | custom-call | flops 2000000000 | bytes 9000000 | tf_op jit(solution)/shard_map/pallas_call | solution.py:265
  57.4 4.6 %all-to-all-start.2 = ((bf16[32,5,8,256]{3,2,1,0:T(8,128)(2,1)}), bf16[32,5,8,256]{3,2,1,0:T(8,128)(2,1)S(1)}, u32[]{:S(2)}, u32[]{:S(2)}) async-start(bf16[32,5,8,256]{3,2,1,0:T(8,128)(2,1)} %shard_map.58), calls=%async_computation.2 | async-start | bytes 1310720 | tf_op jit(solution)/shard_map/all_to_all | solution.py:525
  61.9 10.5 %shard_map.57 = bf16[32,5,8,768]{3,2,1,0:T(8,128)(2,1)} custom-call(bf16[32,5,8,1024]{3,2,1,0:T(8,128)(2,1)S(1)} %all-to-all-done.recv, bf16[4,704,512]{2,1,0:T(8,128)(2,1)} %get-tuple-element.12.inv_any, bf16[4,512,768]{2,1,0:T(8,128)(2,1)} %get-tuple-element.13.direct_any), custom_call_target="tpu_custom_call" | custom-call | flops 6000000000 | bytes 9000000 | tf_op jit(solution)/shard_map/pallas_call | solution.py:265
  72.4 2.6 %all-to-all-done.2.recv = bf16[32,5,8,256]{3,2,1,0:T(8,128)(2,1)S(1)} async-done(((bf16[32,5,8,256]{3,2,1,0:T(8,128)(2,1)}), bf16[32,5,8,256]{3,2,1,0:T(8,128)(2,1)S(1)}, u32[]{:S(2)}, u32[]{:S(2)}) %all-to-all-start.2) | async-done | bytes 655392 | tf_op jit(solution)/shard_map/all_to_all | solution.py:525
  75.0 5.0 %all-to-all-start.1 = ((bf16[32,5,8,768]{3,2,1,0:T(8,128)(2,1)}), bf16[32,5,8,768]{3,2,1,0:T(8,128)(2,1)S(1)}, u32[]{:S(2)}, u32[]{:S(2)}) async-start(bf16[32,5,8,768]{3,2,1,0:T(8,128)(2,1)} %shard_map.57), calls=%async_computation.1 | async-start | bytes 3932160 | tf_op jit(solution)/shard_map/all_to_all | solution.py:525
  80.0 0.3 shard_map.59.rows2
  80.4 1.7 %collective-permute-start.2 = (bf16[10,32,256]{2,1,0:T(8,128)(2,1)S(1)}, bf16[10,32,256]{2,1,0:T(8,128)(2,1)S(1)}, u32[]{:S(2)}, u32[]{:S(2)}) collective-permute-start(bf16[10,32,256]{2,1,0:T(8,128)(2,1)S(1)} %get-tuple-element.23), channel_id=1, source_target_pairs={{0,1},{1,2},{2,3},{3,0},{4,5},{5,6},{6,7},{7,4},{8,9},{9,10},{10,1... | collective-permute-start | bytes 491528 | tf_op jit(solution)/shard_map/ppermute | solution.py:332
  82.1 3.3 %collective-permute-start.1 = (bf16[10,32,256]{2,1,0:T(8,128)(2,1)S(1)}, bf16[10,32,256]{2,1,0:T(8,128)(2,1)S(1)}, u32[]{:S(2)}, u32[]{:S(2)}) collective-permute-start(bf16[10,32,256]{2,1,0:T(8,128)(2,1)S(1)} %get-tuple-element.24), channel_id=1, source_target_pairs={{0,2},{1,3},{2,0},{3,1},{4,6},{5,7},{6,4},{7,5},{8,10},{9,11},{10,... | collective-permute-start | bytes 491528 | tf_op jit(solution)/shard_map/ppermute | solution.py:332
  85.4 0.7 collective-permute-start
  86.2 0.1 fusion.22
  86.3 0.1 fusion.21.matrix
  86.4 2.3 %collective-permute-done.2.r3 = bf16[10,32,256]{2,1,0:T(8,128)(2,1)S(1)} collective-permute-done((bf16[10,32,256]{2,1,0:T(8,128)(2,1)S(1)}, bf16[10,32,256]{2,1,0:T(8,128)(2,1)S(1)}, u32[]{:S(2)}, u32[]{:S(2)}) %collective-permute-start.2) | collective-permute-done | bytes 163872 | tf_op jit(solution)/shard_map/ppermute | solution.py:332
  88.7 4.4 %collective-permute-done.1.r2 = bf16[10,32,256]{2,1,0:T(8,128)(2,1)S(1)} collective-permute-done((bf16[10,32,256]{2,1,0:T(8,128)(2,1)S(1)}, bf16[10,32,256]{2,1,0:T(8,128)(2,1)S(1)}, u32[]{:S(2)}, u32[]{:S(2)}) %collective-permute-start.1) | collective-permute-done | bytes 163872 | tf_op jit(solution)/shard_map/ppermute | solution.py:332
  93.0 0.3 shard_map.60
  93.4 1.2 %collective-permute-start.3 = (bf16[10,32,256]{2,1,0:T(8,128)(2,1)S(1)}, bf16[10,32,256]{2,1,0:T(8,128)(2,1)S(1)}, u32[]{:S(2)}, u32[]{:S(2)}) collective-permute-start(bf16[10,32,256]{2,1,0:T(8,128)(2,1)S(1)} %get-tuple-element.15), channel_id=1, source_target_pairs={{0,1},{1,2},{2,3},{3,0},{4,5},{5,6},{6,7},{7,4},{8,9},{9,10},{10,1... | collective-permute-start | bytes 491528 | tf_op jit(solution)/shard_map/ppermute | solution.py:332
  94.6 2.5 %collective-permute-start.4 = (bf16[10,32,256]{2,1,0:T(8,128)(2,1)S(1)}, bf16[10,32,256]{2,1,0:T(8,128)(2,1)S(1)}, u32[]{:S(2)}, u32[]{:S(2)}) collective-permute-start(bf16[10,32,256]{2,1,0:T(8,128)(2,1)S(1)} %get-tuple-element.16), channel_id=1, source_target_pairs={{0,2},{1,3},{2,0},{3,1},{4,6},{5,7},{6,4},{7,5},{8,10},{9,11},{10,... | collective-permute-start | bytes 491528 | tf_op jit(solution)/shard_map/ppermute | solution.py:332
  97.0 0.1 collective-permute-start.5
  97.1 6.3 %shard_map.61.begun = bf16[10,2,4,32,1281]{4,3,2,1,0:T(8,128)(2,1)} custom-call(s32[320]{0:T(512)S(1)} %copy-done, bf16[4,10,32,256]{3,2,1,0:T(8,128)(2,1)S(1)} %shard_map.59.rows2, bf16[10,1281,256]{2,1,0:T(8,128)(2,1)} %get-tuple-element.18.weight), custom_call_target="tpu_custom_call" | custom-call | flops 2000000000 | bytes 9000000 | tf_op jit(solution)/shard_map/pallas_call | solution.py:426
  103.5 0.9 collective-permute-done.4.c2
  104.4 2.5 %all-to-all-done.1.recv = bf16[32,5,8,768]{3,2,1,0:T(8,128)(2,1)S(1)} async-done(((bf16[32,5,8,768]{3,2,1,0:T(8,128)(2,1)}), bf16[32,5,8,768]{3,2,1,0:T(8,128)(2,1)S(1)}, u32[]{:S(2)}, u32[]{:S(2)}) %all-to-all-start.1) | async-done | bytes 1966112 | tf_op jit(solution)/shard_map/all_to_all | solution.py:525
  106.8 7.8 %shard_map.62 = bf16[10,2,4,32,1281]{4,3,2,1,0:T(8,128)(2,1)} custom-call(s32[320]{0:T(512)S(1)} %copy-done, bf16[32,5,8,768]{3,2,1,0:T(8,128)(2,1)S(1)} %all-to-all-done.1.recv, bf16[10,32,256]{2,1,0:T(8,128)(2,1)S(1)} %get-tuple-element.14.c0, bf16[10,32,256]{2,1,0:T(8,128)(2,1)S(1)} %collective-permute-done.3.c1, ...), custom_call_target="tpu_custom_call", output_to_operand_aliasing={{}: (7, {})} | custom-call | flops 5000000000 | bytes 15000000 | tf_op jit(solution)/shard_map/pallas_call | solution.py:502
  (30 shorter events, 0.6 us)
Async XLA Ops:
  8.7 8.7 %copy-start = (s32[320]{0:T(512)S(1)}, s32[320]{0:T(512)}, u32[]{:S(2)}) copy-start(s32[320]{0:T(512)} %pairs.5) | copy-start | bytes 3844
  8.7 42.5 %all-to-all-start = ((bf16[32,5,8,1024]{3,2,1,0:T(8,128)(2,1)}), bf16[32,5,8,1024]{3,2,1,0:T(8,128)(2,1)S(1)}, u32[]{:S(2)}, u32[]{:S(2)}) async-start(bf16[32,5,8,1024]{3,2,1,0:T(8,128)(2,1)} %shard_map.55), calls=%async_computation | async-start | bytes 5242880 | tf_op jit(solution)/shard_map/all_to_all | solution.py:525
  19.5 7.3 %copy-start.2 = (f32[2048,6]{1,0:T(8,128)S(1)}, f32[2048,6]{1,0:T(8,128)}, u32[]{:S(2)}) copy-start(f32[2048,6]{1,0:T(8,128)} %copy.7) | copy-start | bytes 147460
  20.2 10.5 %copy-start.1 = (f32[256]{0:T(256)S(1)}, f32[256]{0:T(256)}, u32[]{:S(2)}) copy-start(f32[256]{0:T(256)} %param.7) | copy-start | bytes 3076
  57.4 17.6 %all-to-all-start.2 = ((bf16[32,5,8,256]{3,2,1,0:T(8,128)(2,1)}), bf16[32,5,8,256]{3,2,1,0:T(8,128)(2,1)S(1)}, u32[]{:S(2)}, u32[]{:S(2)}) async-start(bf16[32,5,8,256]{3,2,1,0:T(8,128)(2,1)} %shard_map.58), calls=%async_computation.2 | async-start | bytes 1310720 | tf_op jit(solution)/shard_map/all_to_all | solution.py:525
  72.4 13.7 %copy-start.3 = (bf16[128,128]{1,0:T(8,128)(2,1)S(1)}, bf16[128,128]{1,0:T(8,128)(2,1)}, u32[]{:S(2)}) copy-start(bf16[128,128]{1,0:T(8,128)(2,1)} %param.8) | copy-start | bytes 98308
  75.0 31.9 %all-to-all-start.1 = ((bf16[32,5,8,768]{3,2,1,0:T(8,128)(2,1)}), bf16[32,5,8,768]{3,2,1,0:T(8,128)(2,1)S(1)}, u32[]{:S(2)}, u32[]{:S(2)}) async-start(bf16[32,5,8,768]{3,2,1,0:T(8,128)(2,1)} %shard_map.57), calls=%async_computation.1 | async-start | bytes 3932160 | tf_op jit(solution)/shard_map/all_to_all | solution.py:525
  80.4 8.2 %collective-permute-start.2 = (bf16[10,32,256]{2,1,0:T(8,128)(2,1)S(1)}, bf16[10,32,256]{2,1,0:T(8,128)(2,1)S(1)}, u32[]{:S(2)}, u32[]{:S(2)}) collective-permute-start(bf16[10,32,256]{2,1,0:T(8,128)(2,1)S(1)} %get-tuple-element.23), channel_id=1, source_target_pairs={{0,1},{1,2},{2,3},{3,0},{4,5},{5,6},{6,7},{7,4},{8,9},{9,10},{10,1... | collective-permute-start | bytes 491528 | tf_op jit(solution)/shard_map/ppermute | solution.py:332
  82.1 10.9 %collective-permute-start.1 = (bf16[10,32,256]{2,1,0:T(8,128)(2,1)S(1)}, bf16[10,32,256]{2,1,0:T(8,128)(2,1)S(1)}, u32[]{:S(2)}, u32[]{:S(2)}) collective-permute-start(bf16[10,32,256]{2,1,0:T(8,128)(2,1)S(1)} %get-tuple-element.24), channel_id=1, source_target_pairs={{0,2},{1,3},{2,0},{3,1},{4,6},{5,7},{6,4},{7,5},{8,10},{9,11},{10,... | collective-permute-start | bytes 491528 | tf_op jit(solution)/shard_map/ppermute | solution.py:332
  85.4 7.6 %collective-permute-start = (bf16[10,32,256]{2,1,0:T(8,128)(2,1)S(1)}, bf16[10,32,256]{2,1,0:T(8,128)(2,1)S(1)}, u32[]{:S(2)}, u32[]{:S(2)}) collective-permute-start(bf16[10,32,256]{2,1,0:T(8,128)(2,1)S(1)} %get-tuple-element.25), channel_id=1, source_target_pairs={{0,3},{1,0},{2,1},{3,2},{4,7},{5,4},{6,5},{7,6},{8,11},{9,8},{10,9... | collective-permute-start | bytes 491528 | tf_op jit(solution)/shard_map/ppermute | solution.py:332
  93.4 10.1 %collective-permute-start.3 = (bf16[10,32,256]{2,1,0:T(8,128)(2,1)S(1)}, bf16[10,32,256]{2,1,0:T(8,128)(2,1)S(1)}, u32[]{:S(2)}, u32[]{:S(2)}) collective-permute-start(bf16[10,32,256]{2,1,0:T(8,128)(2,1)S(1)} %get-tuple-element.15), channel_id=1, source_target_pairs={{0,1},{1,2},{2,3},{3,0},{4,5},{5,6},{6,7},{7,4},{8,9},{9,10},{10,1... | collective-permute-start | bytes 491528 | tf_op jit(solution)/shard_map/ppermute | solution.py:332
  94.6 9.8 %collective-permute-start.4 = (bf16[10,32,256]{2,1,0:T(8,128)(2,1)S(1)}, bf16[10,32,256]{2,1,0:T(8,128)(2,1)S(1)}, u32[]{:S(2)}, u32[]{:S(2)}) collective-permute-start(bf16[10,32,256]{2,1,0:T(8,128)(2,1)S(1)} %get-tuple-element.16), channel_id=1, source_target_pairs={{0,2},{1,3},{2,0},{3,1},{4,6},{5,7},{6,4},{7,5},{8,10},{9,11},{10,... | collective-permute-start | bytes 491528 | tf_op jit(solution)/shard_map/ppermute | solution.py:332
  97.0 7.3 %collective-permute-start.5 = (bf16[10,32,256]{2,1,0:T(8,128)(2,1)S(1)}, bf16[10,32,256]{2,1,0:T(8,128)(2,1)S(1)}, u32[]{:S(2)}, u32[]{:S(2)}) collective-permute-start(bf16[10,32,256]{2,1,0:T(8,128)(2,1)S(1)} %get-tuple-element.17), channel_id=1, source_target_pairs={{0,3},{1,0},{2,1},{3,2},{4,7},{5,4},{6,5},{7,6},{8,11},{9,8},{10,9... | collective-permute-start | bytes 491528 | tf_op jit(solution)/shard_map/ppermute | solution.py:332

commit v2 on v1

--- a/solution.py
+++ b/solution.py
@@ -35,14 +35,6 @@
 
 def dot_t(a, b):
     return lax.dot_general(a, b, (((1,), (1,)), ((), ())), preferred_element_type=F32)
-
-
-def swap_matrix(outer, inner):
-    n = outer * inner
-    row = lax.broadcasted_iota(jnp.int32, (n, n), 0)
-    col = lax.broadcasted_iota(jnp.int32, (n, n), 1)
-    source = (row % outer) * inner + row // outer
-    return jnp.where(col == source, 1.0, 0.0).astype(F32).astype(BF16)
 
 
 def inverse_kernel(pairs, spec, leg, out, coeffs, legs, store, moved, sem, out_sem):
@@ -89,14 +81,13 @@
                 store[2 * e + c, s] = half[c * 128 : (c + 1) * 128].reshape(FLD, LV, NLAT)
         return carry
 
-    perm = swap_matrix(8, LV)
     leave = [
         pltpu.make_async_copy(moved.at[t], out.at[:, t], out_sem.at[t]) for t in range(5)
     ]
 
     def swapped(tile, blocks):
         for f in range(FLD):
-            value = dot(perm, blocks(f)).reshape(LV, 8, NLAT).astype(BF16)
+            value = pltpu.einshape('slj->lsj', blocks(f).reshape(8, LV, NLAT))
             moved[tile, :, :, f * NLAT : (f + 1) * NLAT] = value
         leave[tile].start()
 
@@ -282,10 +273,8 @@
 
 
 def unswap(recv, lanes, write):
-    perm = swap_matrix(LV, 8)
     for t in range(5):
-        tile = recv[:, t, :, lanes].astype(F32).reshape(8 * LV, NLAT).astype(BF16)
-        moved = dot(perm, tile).astype(BF16).reshape(8, LV, NLAT)
+        moved = pltpu.einshape('lsj->slj', recv[:, t, :, lanes])
         for r in range(8):
             if t < 4:
                 write(t, r, moved[r])

time: 115 us -> 114 us (level)
  Pallas kernels: 52.8 us -> 51.6 us
where the time goes in v2:
time: 114 us
  Pallas kernels  51.6 us (45%)
  starting transfers between devices  27.6 us (24%)
  waiting for transfers between devices  20.6 us (18%)
  other arithmetic  11.5 us (10%)
  local copies, waits for them, and re-layouts  1.97 us (2%)
    all_to_all x3, starting transfers between devices, exchange(): lax.all_to_all(value, 'wave', split_axis=0, concat_axis=0, tiled=True)  18.1 us
    pallas_call x2, Pallas kernels, grid_step(): pl.pallas_call(functools.partial(grid_kernel, needed, wanted), in_specs=[...  16.7 us
    all_to_all x3, waiting for transfers between devices, exchange(): lax.all_to_all(value, 'wave', split_axis=0, concat_axis=0, tiled=True)  13.1 us
    pallas_call x1, Pallas kernels, all_tables(): pl.pallas_call(table_kernel, grid=(SLOTS,), in_specs=row_specs + col_spec...  12.7 us
    ppermute x6, starting transfers between devices, moved(): return lax.ppermute(value, 'lev', [(i, (i + shift) % 4) for i in range(4)])  9.52 us
    pallas_call x1, Pallas kernels, inverse_legendre(): pl.pallas_call(inverse_kernel, in_specs=[pl.BlockSpec(memory_space=pltpu....  8.25 us
    ppermute x6, waiting for transfers between devices, moved(): return lax.ppermute(value, 'lev', [(i, (i + shift) % 4) for i in range(4)])  7.52 us
    pallas_call x1, Pallas kernels, rest_result(): pl.pallas_call(rest_kernel, in_specs=[pl.BlockSpec(memory_space=pltpu.SME...  7.16 us
  transfers between devices with their start and end apart: 9, of which 6 were waited for; matrix products, arithmetic and copies ran while one was open for 12% of the time, Pallas kernels for 26%

profile of v2, /device:TPU:1, one launch (start us, length us, event | category | flops | bytes accessed | tf_op | source)
XLA Modules:
  0.0 113.8 jit_solution(6640086822672385232)
XLA Ops:
  0.0 8.2 %shard_map.55 = bf16[32,5,8,1024]{3,2,1,0:T(8,128)(2,1)} custom-call(s32[320]{0:T(512)} %pairs.5, bf16[10,2,4,32,1281]{4,3,2,1,0:T(8,128)(2,1)} %spec.1, bf16[10,1281,256]{2,1,0:T(8,128)(2,1)} %leg.3), custom_call_target="tpu_custom_call" | custom-call | flops 6000000000 | bytes 17000000 | tf_op jit(solution)/shard_map/pallas_call | solution.py:106
  8.3 8.6 %all-to-all-start = ((bf16[32,5,8,1024]{3,2,1,0:T(8,128)(2,1)}), bf16[32,5,8,1024]{3,2,1,0:T(8,128)(2,1)S(1)}, u32[]{:S(2)}, u32[]{:S(2)}) async-start(bf16[32,5,8,1024]{3,2,1,0:T(8,128)(2,1)} %shard_map.55), calls=%async_computation | async-start | bytes 5242880 | tf_op jit(solution)/shard_map/all_to_all | solution.py:514
  17.4 0.1 reshape_reshape.3
  17.6 0.1 fusion.17
  17.8 1.3 %copy.7 = f32[2048,6]{1,0:T(8,128)} copy(f32[2048,6]{0,1:T(8,128)S(1)} %fusion.17) | data formatting | bytes 98304 | tf_op jit(solution)/shard_map/convert_element_type | solution.py:142
  19.1 0.6 fusion.14
  19.8 2.2 %sine_multiply_fusion.1 = (f32[64,2048]{1,0:T(8,128)S(1)}, f32[64,2048]{1,0:T(8,128)S(1)}) fusion(f32[2048]{0:T(1024)S(1)} %bitcast.26, s32[2048]{0:T(1024)S(1)} %bitcast.28, s32[2048]{0:T(1024)S(1)} %bitcast.23), kind=kLoop, calls=%fused_computation.14 | loop fusion | flops 1572864 | bytes 1073152 | tf_op jit(solution)/shard_map/mul | solution.py:148
  22.0 4.5 %sine_multiply_fusion = (f32[2048,128]{1,0:T(8,128)S(1)}, f32[2048,128]{1,0:T(8,128)S(1)}) fusion(f32[2048]{0:T(1024)S(1)} %bitcast.27, s32[2048]{0:T(1024)S(1)} %bitcast.29, s32[2048]{0:T(1024)S(1)} %bitcast.24), kind=kLoop, calls=%fused_computation.3 | loop fusion | flops 3145728 | bytes 2121728 | tf_op jit(solution)/shard_map/mul | solution.py:153
  26.5 3.7 %multiply_sine_fusion = (f32[2048,6]{1,0:T(8,128)S(1)}, f32[2048,6]{1,0:T(8,128)S(1)}) fusion(f32[2048,6]{1,0:T(8,128)S(1)} %copy-done.2), kind=kLoop, calls=%fused_computation.9 | loop fusion | flops 12288 | bytes 147456 | tf_op jit(solution)/shard_map/sin | solution.py:153
  30.2 12.7 %shard_map.56 = (bf16[4,704,512]{2,1,0:T(8,128)(2,1)}, bf16[4,512,768]{2,1,0:T(8,128)(2,1)}, bf16[10,1281,256]{2,1,0:T(8,128)(2,1)}) custom-call(f32[11,2048]{1,0:T(8,128)S(1)} %get-tuple-element.32.ca, f32[11,2048]{1,0:T(8,128)S(1)} %get-tuple-element.31.sa, f32[64,2048]{1,0:T(8,128)S(1)} %get-tuple-element.30.cb, f32[64,2048]{1,0:T(8,128)S(1)} %get-tuple-element.29.sb, ...), custom_call_target="tpu_custom_call" | custom-call | flops 20000000 | bytes 26000000 | tf_op jit(solution)/shard_map/pallas_call | solution.py:183
  42.9 7.9 %all-to-all-done.recv = bf16[32,5,8,1024]{3,2,1,0:T(8,128)(2,1)S(1)} async-done(((bf16[32,5,8,1024]{3,2,1,0:T(8,128)(2,1)}), bf16[32,5,8,1024]{3,2,1,0:T(8,128)(2,1)S(1)}, u32[]{:S(2)}, u32[]{:S(2)}) %all-to-all-start) | async-done | bytes 2621472 | tf_op jit(solution)/shard_map/all_to_all | solution.py:514
  50.8 6.2 %shard_map.58 = bf16[32,5,8,256]{3,2,1,0:T(8,128)(2,1)} custom-call(bf16[32,5,8,1024]{3,2,1,0:T(8,128)(2,1)S(1)} %all-to-all-done.recv, bf16[4,704,512]{2,1,0:T(8,128)(2,1)} %get-tuple-element.12.inv_any, bf16[4,512,768]{2,1,0:T(8,128)(2,1)} %get-tuple-element.13.direct_any), custom_call_target="tpu_custom_call" | custom-call | flops 2000000000 | bytes 9000000 | tf_op jit(solution)/shard_map/pallas_call | solution.py:256
  57.0 4.6 %all-to-all-start.2 = ((bf16[32,5,8,256]{3,2,1,0:T(8,128)(2,1)}), bf16[32,5,8,256]{3,2,1,0:T(8,128)(2,1)S(1)}, u32[]{:S(2)}, u32[]{:S(2)}) async-start(bf16[32,5,8,256]{3,2,1,0:T(8,128)(2,1)} %shard_map.58), calls=%async_computation.2 | async-start | bytes 1310720 | tf_op jit(solution)/shard_map/all_to_all | solution.py:514
  61.5 10.5 %shard_map.57 = bf16[32,5,8,768]{3,2,1,0:T(8,128)(2,1)} custom-call(bf16[32,5,8,1024]{3,2,1,0:T(8,128)(2,1)S(1)} %all-to-all-done.recv, bf16[4,704,512]{2,1,0:T(8,128)(2,1)} %get-tuple-element.12.inv_any, bf16[4,512,768]{2,1,0:T(8,128)(2,1)} %get-tuple-element.13.direct_any), custom_call_target="tpu_custom_call" | custom-call | flops 6000000000 | bytes 9000000 | tf_op jit(solution)/shard_map/pallas_call | solution.py:256
  72.0 2.6 %all-to-all-done.2.recv = bf16[32,5,8,256]{3,2,1,0:T(8,128)(2,1)S(1)} async-done(((bf16[32,5,8,256]{3,2,1,0:T(8,128)(2,1)}), bf16[32,5,8,256]{3,2,1,0:T(8,128)(2,1)S(1)}, u32[]{:S(2)}, u32[]{:S(2)}) %all-to-all-start.2) | async-done | bytes 655392 | tf_op jit(solution)/shard_map/all_to_all | solution.py:514
  74.6 5.0 %all-to-all-start.1 = ((bf16[32,5,8,768]{3,2,1,0:T(8,128)(2,1)}), bf16[32,5,8,768]{3,2,1,0:T(8,128)(2,1)S(1)}, u32[]{:S(2)}, u32[]{:S(2)}) async-start(bf16[32,5,8,768]{3,2,1,0:T(8,128)(2,1)} %shard_map.57), calls=%async_computation.1 | async-start | bytes 3932160 | tf_op jit(solution)/shard_map/all_to_all | solution.py:514
  79.6 0.2 shard_map.59.rows2
  79.8 1.7 %collective-permute-start.2 = (bf16[10,32,256]{2,1,0:T(8,128)(2,1)S(1)}, bf16[10,32,256]{2,1,0:T(8,128)(2,1)S(1)}, u32[]{:S(2)}, u32[]{:S(2)}) collective-permute-start(bf16[10,32,256]{2,1,0:T(8,128)(2,1)S(1)} %get-tuple-element.23), channel_id=1, source_target_pairs={{0,1},{1,2},{2,3},{3,0},{4,5},{5,6},{6,7},{7,4},{8,9},{9,10},{10,1... | collective-permute-start | bytes 491528 | tf_op jit(solution)/shard_map/ppermute | solution.py:321
  81.5 3.3 %collective-permute-start.1 = (bf16[10,32,256]{2,1,0:T(8,128)(2,1)S(1)}, bf16[10,32,256]{2,1,0:T(8,128)(2,1)S(1)}, u32[]{:S(2)}, u32[]{:S(2)}) collective-permute-start(bf16[10,32,256]{2,1,0:T(8,128)(2,1)S(1)} %get-tuple-element.24), channel_id=1, source_target_pairs={{0,2},{1,3},{2,0},{3,1},{4,6},{5,7},{6,4},{7,5},{8,10},{9,11},{10,... | collective-permute-start | bytes 491528 | tf_op jit(solution)/shard_map/ppermute | solution.py:321
  84.8 0.7 collective-permute-start
  85.6 0.1 fusion.22
  85.7 0.1 fusion.21.matrix
  85.8 2.3 %collective-permute-done.2.r3 = bf16[10,32,256]{2,1,0:T(8,128)(2,1)S(1)} collective-permute-done((bf16[10,32,256]{2,1,0:T(8,128)(2,1)S(1)}, bf16[10,32,256]{2,1,0:T(8,128)(2,1)S(1)}, u32[]{:S(2)}, u32[]{:S(2)}) %collective-permute-start.2) | collective-permute-done | bytes 163872 | tf_op jit(solution)/shard_map/ppermute | solution.py:321
  88.1 4.4 %collective-permute-done.1.r2 = bf16[10,32,256]{2,1,0:T(8,128)(2,1)S(1)} collective-permute-done((bf16[10,32,256]{2,1,0:T(8,128)(2,1)S(1)}, bf16[10,32,256]{2,1,0:T(8,128)(2,1)S(1)}, u32[]{:S(2)}, u32[]{:S(2)}) %collective-permute-start.1) | collective-permute-done | bytes 163872 | tf_op jit(solution)/shard_map/ppermute | solution.py:321
  92.4 0.3 shard_map.60
  92.8 1.2 %collective-permute-start.3 = (bf16[10,32,256]{2,1,0:T(8,128)(2,1)S(1)}, bf16[10,32,256]{2,1,0:T(8,128)(2,1)S(1)}, u32[]{:S(2)}, u32[]{:S(2)}) collective-permute-start(bf16[10,32,256]{2,1,0:T(8,128)(2,1)S(1)} %get-tuple-element.15), channel_id=1, source_target_pairs={{0,1},{1,2},{2,3},{3,0},{4,5},{5,6},{6,7},{7,4},{8,9},{9,10},{10,1... | collective-permute-start | bytes 491528 | tf_op jit(solution)/shard_map/ppermute | solution.py:321
  94.0 2.5 %collective-permute-start.4 = (bf16[10,32,256]{2,1,0:T(8,128)(2,1)S(1)}, bf16[10,32,256]{2,1,0:T(8,128)(2,1)S(1)}, u32[]{:S(2)}, u32[]{:S(2)}) collective-permute-start(bf16[10,32,256]{2,1,0:T(8,128)(2,1)S(1)} %get-tuple-element.16), channel_id=1, source_target_pairs={{0,2},{1,3},{2,0},{3,1},{4,6},{5,7},{6,4},{7,5},{8,10},{9,11},{10,... | collective-permute-start | bytes 491528 | tf_op jit(solution)/shard_map/ppermute | solution.py:321
  96.4 0.1 collective-permute-start.5
  96.6 6.3 %shard_map.61.begun = bf16[10,2,4,32,1281]{4,3,2,1,0:T(8,128)(2,1)} custom-call(s32[320]{0:T(512)S(1)} %copy-done, bf16[4,10,32,256]{3,2,1,0:T(8,128)(2,1)S(1)} %shard_map.59.rows2, bf16[10,1281,256]{2,1,0:T(8,128)(2,1)} %get-tuple-element.18.weight), custom_call_target="tpu_custom_call" | custom-call | flops 2000000000 | bytes 9000000 | tf_op jit(solution)/shard_map/pallas_call | solution.py:415
  102.9 0.9 collective-permute-done.4.c2
  103.8 2.7 %all-to-all-done.1.recv = bf16[32,5,8,768]{3,2,1,0:T(8,128)(2,1)S(1)} async-done(((bf16[32,5,8,768]{3,2,1,0:T(8,128)(2,1)}), bf16[32,5,8,768]{3,2,1,0:T(8,128)(2,1)S(1)}, u32[]{:S(2)}, u32[]{:S(2)}) %all-to-all-start.1) | async-done | bytes 1966112 | tf_op jit(solution)/shard_map/all_to_all | solution.py:514
  106.4 7.2 %shard_map.62 = bf16[10,2,4,32,1281]{4,3,2,1,0:T(8,128)(2,1)} custom-call(s32[320]{0:T(512)S(1)} %copy-done, bf16[32,5,8,768]{3,2,1,0:T(8,128)(2,1)S(1)} %all-to-all-done.1.recv, bf16[10,32,256]{2,1,0:T(8,128)(2,1)S(1)} %get-tuple-element.14.c0, bf16[10,32,256]{2,1,0:T(8,128)(2,1)S(1)} %collective-permute-done.3.c1, ...), custom_call_target="tpu_custom_call", output_to_operand_aliasing={{}: (7, {})} | custom-call | flops 5000000000 | bytes 15000000 | tf_op jit(solution)/shard_map/pallas_call | solution.py:491
  (30 shorter events, 0.6 us)
Async XLA Ops:
  8.3 8.7 %copy-start = (s32[320]{0:T(512)S(1)}, s32[320]{0:T(512)}, u32[]{:S(2)}) copy-start(s32[320]{0:T(512)} %pairs.5) | copy-start | bytes 3844
  8.3 42.5 %all-to-all-start = ((bf16[32,5,8,1024]{3,2,1,0:T(8,128)(2,1)}), bf16[32,5,8,1024]{3,2,1,0:T(8,128)(2,1)S(1)}, u32[]{:S(2)}, u32[]{:S(2)}) async-start(bf16[32,5,8,1024]{3,2,1,0:T(8,128)(2,1)} %shard_map.55), calls=%async_computation | async-start | bytes 5242880 | tf_op jit(solution)/shard_map/all_to_all | solution.py:514
  19.1 7.3 %copy-start.2 = (f32[2048,6]{1,0:T(8,128)S(1)}, f32[2048,6]{1,0:T(8,128)}, u32[]{:S(2)}) copy-start(f32[2048,6]{1,0:T(8,128)} %copy.7) | copy-start | bytes 147460
  19.7 10.5 %copy-start.1 = (f32[256]{0:T(256)S(1)}, f32[256]{0:T(256)}, u32[]{:S(2)}) copy-start(f32[256]{0:T(256)} %param.7) | copy-start | bytes 3076
  57.0 17.6 %all-to-all-start.2 = ((bf16[32,5,8,256]{3,2,1,0:T(8,128)(2,1)}), bf16[32,5,8,256]{3,2,1,0:T(8,128)(2,1)S(1)}, u32[]{:S(2)}, u32[]{:S(2)}) async-start(bf16[32,5,8,256]{3,2,1,0:T(8,128)(2,1)} %shard_map.58), calls=%async_computation.2 | async-start | bytes 1310720 | tf_op jit(solution)/shard_map/all_to_all | solution.py:514
  72.0 13.6 %copy-start.3 = (bf16[128,128]{1,0:T(8,128)(2,1)S(1)}, bf16[128,128]{1,0:T(8,128)(2,1)}, u32[]{:S(2)}) copy-start(bf16[128,128]{1,0:T(8,128)(2,1)} %param.8) | copy-start | bytes 98308
  74.6 31.9 %all-to-all-start.1 = ((bf16[32,5,8,768]{3,2,1,0:T(8,128)(2,1)}), bf16[32,5,8,768]{3,2,1,0:T(8,128)(2,1)S(1)}, u32[]{:S(2)}, u32[]{:S(2)}) async-start(bf16[32,5,8,768]{3,2,1,0:T(8,128)(2,1)} %shard_map.57), calls=%async_computation.1 | async-start | bytes 3932160 | tf_op jit(solution)/shard_map/all_to_all | solution.py:514
  79.8 8.2 %collective-permute-start.2 = (bf16[10,32,256]{2,1,0:T(8,128)(2,1)S(1)}, bf16[10,32,256]{2,1,0:T(8,128)(2,1)S(1)}, u32[]{:S(2)}, u32[]{:S(2)}) collective-permute-start(bf16[10,32,256]{2,1,0:T(8,128)(2,1)S(1)} %get-tuple-element.23), channel_id=1, source_target_pairs={{0,1},{1,2},{2,3},{3,0},{4,5},{5,6},{6,7},{7,4},{8,9},{9,10},{10,1... | collective-permute-start | bytes 491528 | tf_op jit(solution)/shard_map/ppermute | solution.py:321
  81.5 10.9 %collective-permute-start.1 = (bf16[10,32,256]{2,1,0:T(8,128)(2,1)S(1)}, bf16[10,32,256]{2,1,0:T(8,128)(2,1)S(1)}, u32[]{:S(2)}, u32[]{:S(2)}) collective-permute-start(bf16[10,32,256]{2,1,0:T(8,128)(2,1)S(1)} %get-tuple-element.24), channel_id=1, source_target_pairs={{0,2},{1,3},{2,0},{3,1},{4,6},{5,7},{6,4},{7,5},{8,10},{9,11},{10,... | collective-permute-start | bytes 491528 | tf_op jit(solution)/shard_map/ppermute | solution.py:321
  84.8 7.6 %collective-permute-start = (bf16[10,32,256]{2,1,0:T(8,128)(2,1)S(1)}, bf16[10,32,256]{2,1,0:T(8,128)(2,1)S(1)}, u32[]{:S(2)}, u32[]{:S(2)}) collective-permute-start(bf16[10,32,256]{2,1,0:T(8,128)(2,1)S(1)} %get-tuple-element.25), channel_id=1, source_target_pairs={{0,3},{1,0},{2,1},{3,2},{4,7},{5,4},{6,5},{7,6},{8,11},{9,8},{10,9... | collective-permute-start | bytes 491528 | tf_op jit(solution)/shard_map/ppermute | solution.py:321
  92.8 10.1 %collective-permute-start.3 = (bf16[10,32,256]{2,1,0:T(8,128)(2,1)S(1)}, bf16[10,32,256]{2,1,0:T(8,128)(2,1)S(1)}, u32[]{:S(2)}, u32[]{:S(2)}) collective-permute-start(bf16[10,32,256]{2,1,0:T(8,128)(2,1)S(1)} %get-tuple-element.15), channel_id=1, source_target_pairs={{0,1},{1,2},{2,3},{3,0},{4,5},{5,6},{6,7},{7,4},{8,9},{9,10},{10,1... | collective-permute-start | bytes 491528 | tf_op jit(solution)/shard_map/ppermute | solution.py:321
  94.0 9.8 %collective-permute-start.4 = (bf16[10,32,256]{2,1,0:T(8,128)(2,1)S(1)}, bf16[10,32,256]{2,1,0:T(8,128)(2,1)S(1)}, u32[]{:S(2)}, u32[]{:S(2)}) collective-permute-start(bf16[10,32,256]{2,1,0:T(8,128)(2,1)S(1)} %get-tuple-element.16), channel_id=1, source_target_pairs={{0,2},{1,3},{2,0},{3,1},{4,6},{5,7},{6,4},{7,5},{8,10},{9,11},{10,... | collective-permute-start | bytes 491528 | tf_op jit(solution)/shard_map/ppermute | solution.py:321
  96.4 7.3 %collective-permute-start.5 = (bf16[10,32,256]{2,1,0:T(8,128)(2,1)S(1)}, bf16[10,32,256]{2,1,0:T(8,128)(2,1)S(1)}, u32[]{:S(2)}, u32[]{:S(2)}) collective-permute-start(bf16[10,32,256]{2,1,0:T(8,128)(2,1)S(1)} %get-tuple-element.17), channel_id=1, source_target_pairs={{0,3},{1,0},{2,1},{3,2},{4,7},{5,4},{6,5},{7,6},{8,11},{9,8},{10,9... | collective-permute-start | bytes 491528 | tf_op jit(solution)/shard_map/ppermute | solution.py:321

commit v3 on v2

--- a/solution.py
+++ b/solution.py
@@ -203,12 +203,20 @@
     )(*rows, *columns, in_hbm(legendre), lat_weight.reshape(1, NLAT))
 
 
-def grid_kernel(needed, wanted, recv, inv_any, direct_any, out, inv, direct, x, v, sem):
+def grid_kernel(needed, wanted, recv, inv_any, direct_any, out, inv, direct, x, v, stage, sem, out_sem):
     get_inv = [
         pltpu.make_async_copy(inv_any.at[q], inv.at[q], sem.at[0, q]) for q in range(4)
     ]
     get_direct = [
         pltpu.make_async_copy(direct_any.at[q], direct.at[q], sem.at[1, q]) for q in range(4)
+    ]
+    leave = [
+        pltpu.make_async_copy(
+            stage.at[:, :, :, pl.ds(i * NLAT, NLAT)],
+            out.at[:, :, :, pl.ds(i * NLAT, NLAT)],
+            out_sem.at[i],
+        )
+        for i in range(len(wanted))
     ]
     for copy in get_inv + get_direct:
         copy.start()
@@ -224,6 +232,7 @@
     sums = {}
     for q in range(4):
         get_inv[q].wait()
+    for q in range(4):
         for i, f in enumerate(needed):
             sums[f, q] = dot(inv[q], x[q, :, i * NLAT : (i + 1) * NLAT])
     grids = {}
@@ -246,24 +255,29 @@
         for q in range(4):
             v[q, KA:KB, lanes] = jnp.zeros((KB - KA, NLAT), BF16)
             pure = dot(direct[q, 0:256, :], v[q, :, lanes]) * scale
-            out[:, q, :, lanes] = pure.reshape(SRC, 8, NLAT).astype(BF16)
+            stage[:, q, :, lanes] = pure.reshape(SRC, 8, NLAT).astype(BF16)
             term = dot(direct[q, 256:512, :], v[q, :, lanes])
             mixed = term if mixed is None else mixed + term
-        out[:, 4, :, lanes] = (mixed * scale).reshape(SRC, 8, NLAT).astype(BF16)
+        stage[:, 4, :, lanes] = (mixed * scale).reshape(SRC, 8, NLAT).astype(BF16)
+        leave[i].start()
+    for copy in leave:
+        copy.wait()
 
 
 def grid_step(needed, wanted, received, inv, direct):
     return pl.pallas_call(
         functools.partial(grid_kernel, needed, wanted),
         in_specs=[VM] + [pl.BlockSpec(memory_space=pl.ANY)] * 2,
-        out_specs=VM,
+        out_specs=pl.BlockSpec(memory_space=pl.ANY),
         out_shape=pltpu.HBM((SRC, 5, 8, len(wanted) * NLAT), BF16),
         scratch_shapes=[
             pltpu.VMEM((4, KA, 512), BF16),
             pltpu.VMEM((4, 512, KB), BF16),
             pltpu.VMEM((4, 512, len(needed) * NLAT), BF16),
             pltpu.VMEM((4, KB, len(wanted) * NLAT), BF16),
+            pltpu.VMEM((SRC, 5, 8, len(wanted) * NLAT), BF16),
             pltpu.SemaphoreType.DMA((2, 4)),
+            pltpu.SemaphoreType.DMA((len(wanted),)),
         ],
         compiler_params=pltpu.CompilerParams(vmem_limit_bytes=(12 + 8 * len(wanted)) * MIB),
         cost_estimate=pl.CostEstimate(

time: 114 us -> 114 us (level)
  no operation moved by 1% of the time
where the time goes in v3:
time: 114 us; the launch traced here: 113 us
  Pallas kernels  51 us (45%)
  starting transfers between devices  27.1 us (24%)
  waiting for transfers between devices  21.1 us (19%)
  other arithmetic  11.5 us (10%)
  local copies, waits for them, and re-layouts  1.97 us (2%)
    all_to_all x3, starting transfers between devices, exchange(): lax.all_to_all(value, 'wave', split_axis=0, concat_axis=0, tiled=True)  17.6 us
    pallas_call x2, Pallas kernels, grid_step(): pl.pallas_call(functools.partial(grid_kernel, needed, wanted), in_specs=[...  16 us
    all_to_all x3, waiting for transfers between devices, exchange(): lax.all_to_all(value, 'wave', split_axis=0, concat_axis=0, tiled=True)  13.6 us
    pallas_call x1, Pallas kernels, all_tables(): pl.pallas_call(table_kernel, grid=(SLOTS,), in_specs=row_specs + col_spec...  12.7 us
    ppermute x6, starting transfers between devices, moved(): return lax.ppermute(value, 'lev', [(i, (i + shift) % 4) for i in range(4)])  9.52 us
    pallas_call x1, Pallas kernels, inverse_legendre(): pl.pallas_call(inverse_kernel, in_specs=[pl.BlockSpec(memory_space=pltpu....  8.25 us
    ppermute x6, waiting for transfers between devices, moved(): return lax.ppermute(value, 'lev', [(i, (i + shift) % 4) for i in range(4)])  7.51 us
    pallas_call x1, Pallas kernels, rest_result(): pl.pallas_call(rest_kernel, in_specs=[pl.BlockSpec(memory_space=pltpu.SME...  7.16 us
  transfers between devices with their start and end apart: 9, of which 6 were waited for; matrix products, arithmetic and copies ran while one was open for 12% of the time, Pallas kernels for 26%

profile of v3, /device:TPU:1, one launch (start us, length us, event | category | flops | bytes accessed | tf_op | source)
XLA Modules:
  0.0 113.2 jit_solution(1814895399991185355)
XLA Ops:
  0.0 8.2 %shard_map.55 = bf16[32,5,8,1024]{3,2,1,0:T(8,128)(2,1)} custom-call(s32[320]{0:T(512)} %pairs.5, bf16[10,2,4,32,1281]{4,3,2,1,0:T(8,128)(2,1)} %spec.1, bf16[10,1281,256]{2,1,0:T(8,128)(2,1)} %leg.3), custom_call_target="tpu_custom_call" | custom-call | flops 6000000000 | bytes 17000000 | tf_op jit(solution)/shard_map/pallas_call | solution.py:106
  8.3 8.6 %all-to-all-start = ((bf16[32,5,8,1024]{3,2,1,0:T(8,128)(2,1)}), bf16[32,5,8,1024]{3,2,1,0:T(8,128)(2,1)S(1)}, u32[]{:S(2)}, u32[]{:S(2)}) async-start(bf16[32,5,8,1024]{3,2,1,0:T(8,128)(2,1)} %shard_map.55), calls=%async_computation | async-start | bytes 5242880 | tf_op jit(solution)/shard_map/all_to_all | solution.py:528
  17.4 0.1 reshape_reshape.3
  17.6 0.1 fusion.17
  17.8 1.3 %copy.7 = f32[2048,6]{1,0:T(8,128)} copy(f32[2048,6]{0,1:T(8,128)S(1)} %fusion.17) | data formatting | bytes 98304 | tf_op jit(solution)/shard_map/convert_element_type | solution.py:142
  19.1 0.6 fusion.14
  19.8 2.2 %sine_multiply_fusion.1 = (f32[64,2048]{1,0:T(8,128)S(1)}, f32[64,2048]{1,0:T(8,128)S(1)}) fusion(f32[2048]{0:T(1024)S(1)} %bitcast.26, s32[2048]{0:T(1024)S(1)} %bitcast.28, s32[2048]{0:T(1024)S(1)} %bitcast.23), kind=kLoop, calls=%fused_computation.14 | loop fusion | flops 1572864 | bytes 1073152 | tf_op jit(solution)/shard_map/mul | solution.py:148
  22.0 4.5 %sine_multiply_fusion = (f32[2048,128]{1,0:T(8,128)S(1)}, f32[2048,128]{1,0:T(8,128)S(1)}) fusion(f32[2048]{0:T(1024)S(1)} %bitcast.27, s32[2048]{0:T(1024)S(1)} %bitcast.29, s32[2048]{0:T(1024)S(1)} %bitcast.24), kind=kLoop, calls=%fused_computation.3 | loop fusion | flops 3145728 | bytes 2121728 | tf_op jit(solution)/shard_map/mul | solution.py:153
  26.5 3.7 %multiply_sine_fusion = (f32[2048,6]{1,0:T(8,128)S(1)}, f32[2048,6]{1,0:T(8,128)S(1)}) fusion(f32[2048,6]{1,0:T(8,128)S(1)} %copy-done.2), kind=kLoop, calls=%fused_computation.9 | loop fusion | flops 12288 | bytes 147456 | tf_op jit(solution)/shard_map/sin | solution.py:153
  30.2 12.7 %shard_map.56 = (bf16[4,704,512]{2,1,0:T(8,128)(2,1)}, bf16[4,512,768]{2,1,0:T(8,128)(2,1)}, bf16[10,1281,256]{2,1,0:T(8,128)(2,1)}) custom-call(f32[11,2048]{1,0:T(8,128)S(1)} %get-tuple-element.32.ca, f32[11,2048]{1,0:T(8,128)S(1)} %get-tuple-element.31.sa, f32[64,2048]{1,0:T(8,128)S(1)} %get-tuple-element.30.cb, f32[64,2048]{1,0:T(8,128)S(1)} %get-tuple-element.29.sb, ...), custom_call_target="tpu_custom_call" | custom-call | flops 20000000 | bytes 26000000 | tf_op jit(solution)/shard_map/pallas_call | solution.py:183
  42.9 7.9 %all-to-all-done.recv = bf16[32,5,8,1024]{3,2,1,0:T(8,128)(2,1)S(1)} async-done(((bf16[32,5,8,1024]{3,2,1,0:T(8,128)(2,1)}), bf16[32,5,8,1024]{3,2,1,0:T(8,128)(2,1)S(1)}, u32[]{:S(2)}, u32[]{:S(2)}) %all-to-all-start) | async-done | bytes 2621472 | tf_op jit(solution)/shard_map/all_to_all | solution.py:528
  50.8 6.1 %shard_map.58 = bf16[32,5,8,256]{3,2,1,0:T(8,128)(2,1)} custom-call(bf16[32,5,8,1024]{3,2,1,0:T(8,128)(2,1)S(1)} %all-to-all-done.recv, bf16[4,704,512]{2,1,0:T(8,128)(2,1)} %get-tuple-element.12.inv_any, bf16[4,512,768]{2,1,0:T(8,128)(2,1)} %get-tuple-element.13.direct_any), custom_call_target="tpu_custom_call" | custom-call | flops 2000000000 | bytes 9000000 | tf_op jit(solution)/shard_map/pallas_call | solution.py:268
  56.9 4.5 %all-to-all-start.2 = ((bf16[32,5,8,256]{3,2,1,0:T(8,128)(2,1)}), bf16[32,5,8,256]{3,2,1,0:T(8,128)(2,1)S(1)}, u32[]{:S(2)}, u32[]{:S(2)}) async-start(bf16[32,5,8,256]{3,2,1,0:T(8,128)(2,1)} %shard_map.58), calls=%async_computation.2 | async-start | bytes 1310720 | tf_op jit(solution)/shard_map/all_to_all | solution.py:528
  61.4 10.0 %shard_map.57 = bf16[32,5,8,768]{3,2,1,0:T(8,128)(2,1)} custom-call(bf16[32,5,8,1024]{3,2,1,0:T(8,128)(2,1)S(1)} %all-to-all-done.recv, bf16[4,704,512]{2,1,0:T(8,128)(2,1)} %get-tuple-element.12.inv_any, bf16[4,512,768]{2,1,0:T(8,128)(2,1)} %get-tuple-element.13.direct_any), custom_call_target="tpu_custom_call" | custom-call | flops 6000000000 | bytes 9000000 | tf_op jit(solution)/shard_map/pallas_call | solution.py:268
  71.4 3.1 %all-to-all-done.2.recv = bf16[32,5,8,256]{3,2,1,0:T(8,128)(2,1)S(1)} async-done(((bf16[32,5,8,256]{3,2,1,0:T(8,128)(2,1)}), bf16[32,5,8,256]{3,2,1,0:T(8,128)(2,1)S(1)}, u32[]{:S(2)}, u32[]{:S(2)}) %all-to-all-start.2) | async-done | bytes 655392 | tf_op jit(solution)/shard_map/all_to_all | solution.py:528
  74.5 4.4 %all-to-all-start.1 = ((bf16[32,5,8,768]{3,2,1,0:T(8,128)(2,1)}), bf16[32,5,8,768]{3,2,1,0:T(8,128)(2,1)S(1)}, u32[]{:S(2)}, u32[]{:S(2)}) async-start(bf16[32,5,8,768]{3,2,1,0:T(8,128)(2,1)} %shard_map.57), calls=%async_computation.1 | async-start | bytes 3932160 | tf_op jit(solution)/shard_map/all_to_all | solution.py:528
  79.0 0.2 shard_map.59.rows2
  79.2 1.7 %collective-permute-start.2 = (bf16[10,32,256]{2,1,0:T(8,128)(2,1)S(1)}, bf16[10,32,256]{2,1,0:T(8,128)(2,1)S(1)}, u32[]{:S(2)}, u32[]{:S(2)}) collective-permute-start(bf16[10,32,256]{2,1,0:T(8,128)(2,1)S(1)} %get-tuple-element.23), channel_id=1, source_target_pairs={{0,1},{1,2},{2,3},{3,0},{4,5},{5,6},{6,7},{7,4},{8,9},{9,10},{10,1... | collective-permute-start | bytes 491528 | tf_op jit(solution)/shard_map/ppermute | solution.py:335
  80.9 3.3 %collective-permute-start.1 = (bf16[10,32,256]{2,1,0:T(8,128)(2,1)S(1)}, bf16[10,32,256]{2,1,0:T(8,128)(2,1)S(1)}, u32[]{:S(2)}, u32[]{:S(2)}) collective-permute-start(bf16[10,32,256]{2,1,0:T(8,128)(2,1)S(1)} %get-tuple-element.24), channel_id=1, source_target_pairs={{0,2},{1,3},{2,0},{3,1},{4,6},{5,7},{6,4},{7,5},{8,10},{9,11},{10,... | collective-permute-start | bytes 491528 | tf_op jit(solution)/shard_map/ppermute | solution.py:335
  84.2 0.7 collective-permute-start
  84.9 0.1 fusion.22
  85.1 0.1 fusion.21.matrix
  85.2 2.3 %collective-permute-done.2.r3 = bf16[10,32,256]{2,1,0:T(8,128)(2,1)S(1)} collective-permute-done((bf16[10,32,256]{2,1,0:T(8,128)(2,1)S(1)}, bf16[10,32,256]{2,1,0:T(8,128)(2,1)S(1)}, u32[]{:S(2)}, u32[]{:S(2)}) %collective-permute-start.2) | collective-permute-done | bytes 163872 | tf_op jit(solution)/shard_map/ppermute | solution.py:335
  87.5 4.4 %collective-permute-done.1.r2 = bf16[10,32,256]{2,1,0:T(8,128)(2,1)S(1)} collective-permute-done((bf16[10,32,256]{2,1,0:T(8,128)(2,1)S(1)}, bf16[10,32,256]{2,1,0:T(8,128)(2,1)S(1)}, u32[]{:S(2)}, u32[]{:S(2)}) %collective-permute-start.1) | collective-permute-done | bytes 163872 | tf_op jit(solution)/shard_map/ppermute | solution.py:335
  91.8 0.3 shard_map.60
  92.2 1.2 %collective-permute-start.3 = (bf16[10,32,256]{2,1,0:T(8,128)(2,1)S(1)}, bf16[10,32,256]{2,1,0:T(8,128)(2,1)S(1)}, u32[]{:S(2)}, u32[]{:S(2)}) collective-permute-start(bf16[10,32,256]{2,1,0:T(8,128)(2,1)S(1)} %get-tuple-element.15), channel_id=1, source_target_pairs={{0,1},{1,2},{2,3},{3,0},{4,5},{5,6},{6,7},{7,4},{8,9},{9,10},{10,1... | collective-permute-start | bytes 491528 | tf_op jit(solution)/shard_map/ppermute | solution.py:335
  93.4 2.5 %collective-permute-start.4 = (bf16[10,32,256]{2,1,0:T(8,128)(2,1)S(1)}, bf16[10,32,256]{2,1,0:T(8,128)(2,1)S(1)}, u32[]{:S(2)}, u32[]{:S(2)}) collective-permute-start(bf16[10,32,256]{2,1,0:T(8,128)(2,1)S(1)} %get-tuple-element.16), channel_id=1, source_target_pairs={{0,2},{1,3},{2,0},{3,1},{4,6},{5,7},{6,4},{7,5},{8,10},{9,11},{10,... | collective-permute-start | bytes 491528 | tf_op jit(solution)/shard_map/ppermute | solution.py:335
  95.8 0.1 collective-permute-start.5
  95.9 6.3 %shard_map.61.begun = bf16[10,2,4,32,1281]{4,3,2,1,0:T(8,128)(2,1)} custom-call(s32[320]{0:T(512)S(1)} %copy-done, bf16[4,10,32,256]{3,2,1,0:T(8,128)(2,1)S(1)} %shard_map.59.rows2, bf16[10,1281,256]{2,1,0:T(8,128)(2,1)} %get-tuple-element.18.weight), custom_call_target="tpu_custom_call" | custom-call | flops 2000000000 | bytes 9000000 | tf_op jit(solution)/shard_map/pallas_call | solution.py:429
  102.3 0.9 collective-permute-done.4.c2
  103.2 2.7 %all-to-all-done.1.recv = bf16[32,5,8,768]{3,2,1,0:T(8,128)(2,1)S(1)} async-done(((bf16[32,5,8,768]{3,2,1,0:T(8,128)(2,1)}), bf16[32,5,8,768]{3,2,1,0:T(8,128)(2,1)S(1)}, u32[]{:S(2)}, u32[]{:S(2)}) %all-to-all-start.1) | async-done | bytes 1966112 | tf_op jit(solution)/shard_map/all_to_all | solution.py:528
  105.8 7.2 %shard_map.62 = bf16[10,2,4,32,1281]{4,3,2,1,0:T(8,128)(2,1)} custom-call(s32[320]{0:T(512)S(1)} %copy-done, bf16[32,5,8,768]{3,2,1,0:T(8,128)(2,1)S(1)} %all-to-all-done.1.recv, bf16[10,32,256]{2,1,0:T(8,128)(2,1)S(1)} %get-tuple-element.14.c0, bf16[10,32,256]{2,1,0:T(8,128)(2,1)S(1)} %collective-permute-done.3.c1, ...), custom_call_target="tpu_custom_call", output_to_operand_aliasing={{}: (7, {})} | custom-call | flops 5000000000 | bytes 15000000 | tf_op jit(solution)/shard_map/pallas_call | solution.py:505
  (30 shorter events, 0.6 us)
Async XLA Ops:
  8.3 8.7 %copy-start = (s32[320]{0:T(512)S(1)}, s32[320]{0:T(512)}, u32[]{:S(2)}) copy-start(s32[320]{0:T(512)} %pairs.5) | copy-start | bytes 3844
  8.3 42.5 %all-to-all-start = ((bf16[32,5,8,1024]{3,2,1,0:T(8,128)(2,1)}), bf16[32,5,8,1024]{3,2,1,0:T(8,128)(2,1)S(1)}, u32[]{:S(2)}, u32[]{:S(2)}) async-start(bf16[32,5,8,1024]{3,2,1,0:T(8,128)(2,1)} %shard_map.55), calls=%async_computation | async-start | bytes 5242880 | tf_op jit(solution)/shard_map/all_to_all | solution.py:528
  19.1 7.3 %copy-start.2 = (f32[2048,6]{1,0:T(8,128)S(1)}, f32[2048,6]{1,0:T(8,128)}, u32[]{:S(2)}) copy-start(f32[2048,6]{1,0:T(8,128)} %copy.7) | copy-start | bytes 147460
  19.7 10.5 %copy-start.1 = (f32[256]{0:T(256)S(1)}, f32[256]{0:T(256)}, u32[]{:S(2)}) copy-start(f32[256]{0:T(256)} %param.7) | copy-start | bytes 3076
  56.9 17.6 %all-to-all-start.2 = ((bf16[32,5,8,256]{3,2,1,0:T(8,128)(2,1)}), bf16[32,5,8,256]{3,2,1,0:T(8,128)(2,1)S(1)}, u32[]{:S(2)}, u32[]{:S(2)}) async-start(bf16[32,5,8,256]{3,2,1,0:T(8,128)(2,1)} %shard_map.58), calls=%async_computation.2 | async-start | bytes 1310720 | tf_op jit(solution)/shard_map/all_to_all | solution.py:528
  71.4 13.6 %copy-start.3 = (bf16[128,128]{1,0:T(8,128)(2,1)S(1)}, bf16[128,128]{1,0:T(8,128)(2,1)}, u32[]{:S(2)}) copy-start(bf16[128,128]{1,0:T(8,128)(2,1)} %param.8) | copy-start | bytes 98308
  74.5 31.3 %all-to-all-start.1 = ((bf16[32,5,8,768]{3,2,1,0:T(8,128)(2,1)}), bf16[32,5,8,768]{3,2,1,0:T(8,128)(2,1)S(1)}, u32[]{:S(2)}, u32[]{:S(2)}) async-start(bf16[32,5,8,768]{3,2,1,0:T(8,128)(2,1)} %shard_map.57), calls=%async_computation.1 | async-start | bytes 3932160 | tf_op jit(solution)/shard_map/all_to_all | solution.py:528
  79.2 8.2 %collective-permute-start.2 = (bf16[10,32,256]{2,1,0:T(8,128)(2,1)S(1)}, bf16[10,32,256]{2,1,0:T(8,128)(2,1)S(1)}, u32[]{:S(2)}, u32[]{:S(2)}) collective-permute-start(bf16[10,32,256]{2,1,0:T(8,128)(2,1)S(1)} %get-tuple-element.23), channel_id=1, source_target_pairs={{0,1},{1,2},{2,3},{3,0},{4,5},{5,6},{6,7},{7,4},{8,9},{9,10},{10,1... | collective-permute-start | bytes 491528 | tf_op jit(solution)/shard_map/ppermute | solution.py:335
  80.9 10.9 %collective-permute-start.1 = (bf16[10,32,256]{2,1,0:T(8,128)(2,1)S(1)}, bf16[10,32,256]{2,1,0:T(8,128)(2,1)S(1)}, u32[]{:S(2)}, u32[]{:S(2)}) collective-permute-start(bf16[10,32,256]{2,1,0:T(8,128)(2,1)S(1)} %get-tuple-element.24), channel_id=1, source_target_pairs={{0,2},{1,3},{2,0},{3,1},{4,6},{5,7},{6,4},{7,5},{8,10},{9,11},{10,... | collective-permute-start | bytes 491528 | tf_op jit(solution)/shard_map/ppermute | solution.py:335
  84.2 7.6 %collective-permute-start = (bf16[10,32,256]{2,1,0:T(8,128)(2,1)S(1)}, bf16[10,32,256]{2,1,0:T(8,128)(2,1)S(1)}, u32[]{:S(2)}, u32[]{:S(2)}) collective-permute-start(bf16[10,32,256]{2,1,0:T(8,128)(2,1)S(1)} %get-tuple-element.25), channel_id=1, source_target_pairs={{0,3},{1,0},{2,1},{3,2},{4,7},{5,4},{6,5},{7,6},{8,11},{9,8},{10,9... | collective-permute-start | bytes 491528 | tf_op jit(solution)/shard_map/ppermute | solution.py:335
  92.2 10.1 %collective-permute-start.3 = (bf16[10,32,256]{2,1,0:T(8,128)(2,1)S(1)}, bf16[10,32,256]{2,1,0:T(8,128)(2,1)S(1)}, u32[]{:S(2)}, u32[]{:S(2)}) collective-permute-start(bf16[10,32,256]{2,1,0:T(8,128)(2,1)S(1)} %get-tuple-element.15), channel_id=1, source_target_pairs={{0,1},{1,2},{2,3},{3,0},{4,5},{5,6},{6,7},{7,4},{8,9},{9,10},{10,1... | collective-permute-start | bytes 491528 | tf_op jit(solution)/shard_map/ppermute | solution.py:335
  93.4 9.8 %collective-permute-start.4 = (bf16[10,32,256]{2,1,0:T(8,128)(2,1)S(1)}, bf16[10,32,256]{2,1,0:T(8,128)(2,1)S(1)}, u32[]{:S(2)}, u32[]{:S(2)}) collective-permute-start(bf16[10,32,256]{2,1,0:T(8,128)(2,1)S(1)} %get-tuple-element.16), channel_id=1, source_target_pairs={{0,2},{1,3},{2,0},{3,1},{4,6},{5,7},{6,4},{7,5},{8,10},{9,11},{10,... | collective-permute-start | bytes 491528 | tf_op jit(solution)/shard_map/ppermute | solution.py:335
  95.8 7.3 %collective-permute-start.5 = (bf16[10,32,256]{2,1,0:T(8,128)(2,1)S(1)}, bf16[10,32,256]{2,1,0:T(8,128)(2,1)S(1)}, u32[]{:S(2)}, u32[]{:S(2)}) collective-permute-start(bf16[10,32,256]{2,1,0:T(8,128)(2,1)S(1)} %get-tuple-element.17), channel_id=1, source_target_pairs={{0,3},{1,0},{2,1},{3,2},{4,7},{5,4},{6,5},{7,6},{8,11},{9,8},{10,9... | collective-permute-start | bytes 491528 | tf_op jit(solution)/shard_map/ppermute | solution.py:335
